TPU v7x, 256 devices: a whole 4x4x8 slice. The times are simulated.
256 devices in a mesh: seq: 8 (over y, core), tp: 8 (over z), dp: 4 (over x).
Axes of the slice: x: 4, y: 4, z: 8, core: 2. Of those that a mesh axis runs over, the one named last changes fastest.
Arguments:
- queries: bfloat16 [16384, 4096], P(('seq', 'dp'), 'tp'), may hold values from -6 to 6
- keys: bfloat16 [16384, 4096], P(('seq', 'dp'), 'tp'), may hold values from -6 to 6
- values: bfloat16 [16384, 4096], P(('seq', 'dp'), 'tp'), may hold values from -6 to 6
- gain: float32 [4096], P('tp'), may hold values from 0.5 to 2
- out_weight: bfloat16 [4096, 4096], P(('seq', 'dp'), 'tp'), may hold values from -0.09375 to 0.09375
- out_cotangent: bfloat16 [16384, 4096], P(('seq', 'dp'), 'tp'), may hold values from -6 to 6
Outputs:
- query_grad: bfloat16 [16384, 4096], P(('seq', 'dp'), 'tp')
- key_grad: bfloat16 [16384, 4096], P(('seq', 'dp'), 'tp')
- value_grad: bfloat16 [16384, 4096], P(('seq', 'dp'), 'tp')
- gain_grad: float32 [4096], P('tp')
- weight_grad: float32 [4096, 4096], P(('seq', 'dp'), 'tp')
All inputs are finite; a program needn't handle non-finite values.
Results may differ from a plain program's by a relative error of at most 0.023.
Values may be sent and summed in bfloat16 or wider, within the bound.
No kernel may reach another device: no remote copies, remote signals or barrier semaphores. Data moves between devices by JAX's collectives and lax.ppermute only.
A program may use at most 128 MiB of HBM per device.

v0:
```python
import math

import jax
import jax.numpy as jnp
from jax import lax
from jax.sharding import PartitionSpec as P

HEAD_DIM = 128


EPS = 1e-06


def entering(shard, axis, join, neutral, backward):
    count = lax.axis_size(axis)
    place = lax.axis_index(axis)
    ahead = count - 1 - place if backward else place
    gathered = lax.all_gather(shard.astype(jnp.bfloat16), axis)
    state = jnp.zeros_like(shard) + jnp.asarray(neutral, shard.dtype)

    def one(turn, state):
        source = count - 1 - turn if backward else turn
        return join(state, lax.dynamic_index_in_dim(gathered, source, 0, False).astype(shard.dtype))

    return lax.fori_loop(0, ahead, one, state)


def add_pair(earlier, latter):
    return earlier + latter


def body(queries, keys, values, gain, out_weight, out_cotangent):
    length = queries.shape[0]
    local_width = queries.shape[1]
    local_heads = local_width // HEAD_DIM
    bfloat = jnp.bfloat16
    single = jnp.float32
    query_h = queries.reshape(length, local_heads, HEAD_DIM)
    key_h = keys.reshape(length, local_heads, HEAD_DIM)
    value_h = values.reshape(length, local_heads, HEAD_DIM)
    positions = lax.iota(jnp.int32, length)
    causal = positions[:, None] >= positions[None, :]
    local_state = jnp.einsum("thi,thj->hij", key_h, value_h, preferred_element_type=single)
    empty_state = jnp.zeros_like(local_state)
    prior_sum = entering(local_state, ("seq", "dp"), add_pair, empty_state, False)
    prior_state = prior_sum.astype(bfloat)
    scores = jnp.einsum("thi,shi->hts", query_h, key_h, preferred_element_type=single)
    scores = jnp.where(causal, scores, 0.0).astype(bfloat)
    attended = jnp.einsum("hts,shj->thj", scores, value_h, preferred_element_type=single)
    attended = attended + jnp.einsum(
        "thi,hij->thj", query_h, prior_state, preferred_element_type=single
    )
    inverse_rms = lax.rsqrt(jnp.mean(attended * attended, axis=-1, keepdims=True) + EPS)
    normed = attended * inverse_rms
    gain_view = gain.reshape(local_heads, HEAD_DIM)
    gated = (normed * gain_view).reshape(length, local_width).astype(bfloat)
    full_rows = lax.all_gather(out_cotangent, "tp", axis=1, tiled=True)
    columns = full_rows
    grad_gated = jnp.dot(
        columns,
        lax.all_gather(out_weight, ("seq", "dp"), axis=0, tiled=True),
        preferred_element_type=single,
    )
    token_total = length * lax.axis_size("seq") * lax.axis_size("dp")
    grad_scale = 1.0 / math.sqrt(token_total)
    gain_local = jnp.sum(grad_gated * normed.reshape(length, local_width), axis=0)
    gain_grad = lax.psum(gain_local, ("seq", "dp")) * grad_scale
    columns = full_rows
    weight_sum = lax.psum_scatter(
        lax.dot_general(
            columns, gated, (((0,), (0,)), ((), ())), preferred_element_type=single
        ).astype(jnp.bfloat16),
        ("seq", "dp"),
        scatter_dimension=0,
        tiled=True,
    ).astype(jnp.float32)
    weight_grad = weight_sum * grad_scale
    grad_normed = grad_gated.reshape(length, local_heads, HEAD_DIM) * gain_view
    grad_attended = (
        grad_normed - normed * jnp.mean(grad_normed * normed, axis=-1, keepdims=True)
    ) * inverse_rms
    grad_attended = grad_attended.astype(bfloat)
    back_scores = jnp.einsum("thj,shj->hts", grad_attended, value_h, preferred_element_type=single)
    back_scores = jnp.where(causal, back_scores, 0.0).astype(bfloat)
    grad_state = jnp.einsum("thi,thj->hij", query_h, grad_attended, preferred_element_type=single)
    later_sum = entering(grad_state, ("seq", "dp"), add_pair, empty_state, True)
    later_state = later_sum.astype(bfloat)
    query_grad = jnp.einsum("hts,shi->thi", back_scores, key_h, preferred_element_type=single)
    query_grad = query_grad + jnp.einsum(
        "thj,hij->thi", grad_attended, prior_state, preferred_element_type=single
    )
    key_grad = jnp.einsum("hts,thi->shi", back_scores, query_h, preferred_element_type=single)
    key_grad = key_grad + jnp.einsum(
        "shj,hij->shi", value_h, later_state, preferred_element_type=single
    )
    value_grad = jnp.einsum("hts,thj->shj", scores, grad_attended, preferred_element_type=single)
    value_grad = value_grad + jnp.einsum(
        "shi,hij->shj", key_h, later_state, preferred_element_type=single
    )
    out_shape = (length, local_width)
    return (
        query_grad.reshape(out_shape).astype(bfloat),
        key_grad.reshape(out_shape).astype(bfloat),
        value_grad.reshape(out_shape).astype(bfloat),
        gain_grad,
        weight_grad,
    )


def solution(mesh):
    return jax.shard_map(
        body,
        mesh=mesh,
        in_specs=(
            P(("seq", "dp"), "tp"),
            P(("seq", "dp"), "tp"),
            P(("seq", "dp"), "tp"),
            P("tp"),
            P(("seq", "dp"), "tp"),
            P(("seq", "dp"), "tp"),
        ),
        out_specs=(
            P(("seq", "dp"), "tp"),
            P(("seq", "dp"), "tp"),
            P(("seq", "dp"), "tp"),
            P("tp"),
            P(("seq", "dp"), "tp"),
        ),
        check_vma=False,
    )
```

profile of v0, /device:TPU:6, one launch (start us, length us, event | category | flops | bytes accessed | tf_op | source)
XLA Modules:
  0.0 359.8 jit_solution(6980432426997382842)
XLA Ops:
  7.2 1.3 copy.102
  8.6 2.2 convolution_convert_fusion.2
  13.1 1.8 select_convert_fusion.1
  14.9 1.3 copy-done.1
  17.1 47.7 %all-gather.11.cloned.1.call-done = bf16[128,128,128]{2,1,0:T(8,128)(2,1)} async-done(((bf16[4,128,128]{2,1,0:T(8,128)(2,1)}), bf16[128,128,128]{2,1,0:T(8,128)(2,1)}) %all-gather.11.cloned.1.call-update) | async-done | bytes 4194320 | tf_op jit(solution)/shard_map/all_gather | solution.py:18
  64.9 3.0 while.22
  68.4 52.9 %all-gather.7.cloned.1.call-done = bf16[512,4096]{1,0:T(8,128)(2,1)} async-done(((bf16[512,512]{1,0:T(8,128)(2,1)}), bf16[512,4096]{1,0:T(8,128)(2,1)}) %all-gather.7.cloned.1.call-update) | async-done | bytes 4194320 | tf_op jit(solution)/shard_map/all_gather | solution.py:57
  121.3 6.5 %fusion = bf16[4096,512]{0,1:T(8,128)(2,1)} fusion(bf16[512,512]{0,1:T(8,128)(2,1)S(1)} %bitcast.131, bf16[512,4096]{1,0:T(8,128)(2,1)} %all-gather.7.cloned.1.call-done), kind=kOutput, calls=%fused_computation.3 | convolution fusion | flops 2149580800 | bytes 8912896 | tf_op jit(solution)/shard_map/dot_general | solution.py:70
  127.7 6.5 %copy.57 = bf16[4096,512]{1,0:T(8,128)(2,1)} copy(bf16[4096,512]{0,1:T(8,128)(2,1)} %fusion) | data formatting | bytes 8388608
  134.3 38.9 %all-gather.9.cloned.1.call-done = bf16[4096,512]{1,0:T(8,128)(2,1)} async-done(((bf16[128,512]{1,0:T(8,128)(2,1)}), bf16[4096,512]{1,0:T(8,128)(2,1)}) %all-gather.9.cloned.1.call-update) | async-done | bytes 4194320 | tf_op jit(solution)/shard_map/all_gather | solution.py:61
  173.2 5.9 %multiply_reduce_fusion = (f32[512,4]{0,1:T(4,128)S(1)}, f32[512,512]{0,1:T(8,128)S(1)}) fusion(f32[512,4,128]{0,2,1:T(8,128)S(1)} %get-tuple-element.117, f32[4,128]{1,0:T(4,128)S(1)} %bitcast.135, bf16[512,4096]{1,0:T(8,128)(2,1)} %all-gather.7.cloned.1.call-done, bf16[4096,512]{1,0:T(8,128)(2,1)} %all-gather.9.cloned.1.call-done), kind=kOutput, calls=%fused_computation.26 | convolution fusion | flops 2148268032 | bytes 10496000 | tf_op jit(solution)/shard_map/dot_general | solution.py:59
  180.4 2.0 select_convert_fusion
  183.3 1.1 fusion.4
  184.3 2.0 copy.49
  186.6 61.2 %psum.7 = f32[512]{0:T(512)S(1)} all-reduce(f32[512]{0:T(512)S(1)} %fusion.8), channel_id=1, replica_groups=mesh['seq'=8,'tp'=8,'dp'=4] {'seq','dp'}, use_global_device_ids=true, to_apply=%region_7.8 | all-reduce | flops 512 | bytes 4096 | tf_op jit(solution)/shard_map/psum | solution.py:67
  248.4 3.0 fusion.33
  251.4 1.6 convolution_bitcast_fusion
  252.9 13.1 %reduce-scatter.4.cloned.1.call-done = bf16[128,512]{1,0:T(8,128)(2,1)} async-done(((bf16[4096,512]{1,0:T(8,128)(2,1)}), bf16[128,512]{1,0:T(8,128)(2,1)}) %reduce-scatter.4.cloned.1.call-update) | async-done | bytes 131088
  266.1 1.0 copy.58
  268.0 51.9 %all-gather.13.cloned.1.call-done = bf16[128,128,128]{2,1,0:T(8,128)(2,1)} async-done(((bf16[4,128,128]{2,1,0:T(8,128)(2,1)}), bf16[128,128,128]{2,1,0:T(8,128)(2,1)}) %all-gather.13.cloned.1.call-update) | async-done | bytes 4194320 | tf_op jit(solution)/shard_map/all_gather | solution.py:18
  319.9 27.8 %while.23 = (s32[]{:T(128)}, f32[4,128,128]{2,1,0:T(8,128)S(1)}, s32[]{:T(128)}, bf16[32,4,128,128]{3,2,1,0:T(8,128)(2,1)}, s32[]{:T(128)}, /*index=5*/s32[]{:T(128)}, s32[]{:T(128)}, s32[]{:T(128)}) while((s32[]{:T(128)}, f32[4,128,128]{2,1,0:T(8,128)S(1)}, s32[]{:T(128)}, bf16[32,4,128,128]{3,2,1,0:T(8,128)(2,1)}, s32[]{:T(128)}, ...), condition=%wide.region_5.6_spmd, body=%wide.region_4.5_spmd.sunk | while | flops 131078 | bytes 655495 | solution.py:25
  347.7 2.2 fusion.6
  349.9 2.0 copy.51
  352.2 1.0 copy.50
  (81 shorter events, 37.7 us)
Async XLA Ops:
  7.2 6.0 %copy-start = (bf16[512,512]{1,0:T(8,128)(2,1)S(1)}, bf16[512,512]{1,0:T(8,128)(2,1)}, u32[]{:S(2)}) copy-start(bf16[512,512]{1,0:T(8,128)(2,1)} %param.10) | copy-start | bytes 1572868
  7.2 9.1 %copy-start.8 = (bf16[512,512]{1,0:T(8,128)(2,1)S(1)}, bf16[512,512]{1,0:T(8,128)(2,1)}, u32[]{:S(2)}) copy-start(bf16[512,512]{1,0:T(8,128)(2,1)} %param.12) | copy-start | bytes 1572868
  7.2 57.6 %all-gather.11.cloned.1.call-start = ((), (), s32[]{:S(2)}) async-start(), calls=%async_computation.3 | async-start | bytes 4325376 | tf_op jit(solution)/shard_map/all_gather | solution.py:18
  8.6 3.8 %copy-start.6 = (bf16[512,512]{0,1:T(8,128)(2,1)}, bf16[512,512]{0,1:T(8,128)(2,1)S(1)}, u32[]{:S(2)}) copy-start(bf16[512,512]{0,1:T(8,128)(2,1)S(1)} %copy.102) | copy-start | bytes 1572868
  10.8 110.5 %all-gather.7.cloned.1.call-start = ((), (), s32[]{:S(2)}) async-start(), calls=%async_computation.1 | async-start | bytes 4718592 | tf_op jit(solution)/shard_map/all_gather | solution.py:57
  11.5 161.7 %all-gather.9.cloned.1.call-start = ((), (), s32[]{:S(2)}) async-start(), calls=%async_computation.2 | async-start | bytes 4325376 | tf_op jit(solution)/shard_map/all_gather | solution.py:61
  12.3 253.8 %reduce-scatter.4.cloned.1.call-start = ((), (), s32[]{:S(2)}) async-start(), calls=%async_computation.5 | async-start | bytes 4325376
  12.4 0.7 copy-start.10
  14.9 1.3 copy-start.1
  17.1 51.1 %copy-start.11 = (f32[512]{0:T(512)S(1)}, f32[512]{0:T(512)}, u32[]{:S(2)}) copy-start(f32[512]{0:T(512)} %param.13) | copy-start | bytes 6148
  134.3 185.6 %all-gather.13.cloned.1.call-start = ((), (), s32[]{:S(2)}) async-start(), calls=%async_computation.4 | async-start | bytes 4325376 | tf_op jit(solution)/shard_map/all_gather | solution.py:18
  180.4 2.0 copy-start.7
  182.4 1.9 copy-start.2
  186.6 64.8 %copy-start.3 = (bf16[4,512,512]{2,1,0:T(8,128)(2,1)S(1)}, bf16[4,512,512]{2,1,0:T(8,128)(2,1)}, u32[]{:S(2)}) copy-start(bf16[4,512,512]{2,1,0:T(8,128)(2,1)} %copy-done.2) | copy-start | bytes 6291460
  252.9 94.7 %copy-start.5 = (f32[4,128,512]{2,1,0:T(8,128)S(1)}, f32[4,128,512]{2,1,0:T(8,128)}, u32[]{:S(2)}) copy-start(f32[4,128,512]{2,1,0:T(8,128)} %fusion.33) | copy-start | bytes 3145732
  252.9 99.0 %copy-start.4 = (f32[512,4,128]{0,2,1:T(8,128)S(1)}, f32[512,4,128]{0,2,1:T(8,128)}, u32[]{:S(2)}) copy-start(f32[512,4,128]{0,2,1:T(8,128)} %convolution_bitcast_fusion) | copy-start | bytes 3145732
  252.9 99.0 %copy-start.9 = (bf16[512,512]{1,0:T(8,128)(2,1)S(1)}, bf16[512,512]{1,0:T(8,128)(2,1)}, u32[]{:S(2)}) copy-start(bf16[512,512]{1,0:T(8,128)(2,1)} %param.12) | copy-start | bytes 1572868
Sparse Core Ops, SparseCore 0:
  11.2 53.6 all-gather.10
  66.6 54.5 all-gather.6
  123.8 49.3 all-gather.8
  177.0 89.0 reduce-scatter.3
  269.4 50.4 all-gather.12
where the time goes:
time: 364 us; the launch traced here: 360 us
  waiting for transfers between devices  206 us (57%)
  blocking collectives  61.2 us (17%)
  other arithmetic  31.1 us (9%)
  matrix products  28.7 us (8%)
  local copies, waits for them, and re-layouts  17.7 us (5%)
  between operations  14 us (4%)
    all_gather x2, waiting for transfers between devices, entering(): gathered = lax.all_gather(shard.astype(jnp.bfloat16), axis)  99.6 us
    psum x1, blocking collectives, body(): gain_grad = lax.psum(gain_local, ('seq', 'dp')) * grad_scale  61.2 us
    all_gather x1, waiting for transfers between devices, body(): full_rows = lax.all_gather(out_cotangent, 'tp', axis=1, tiled=True)  52.9 us
    all_gather x1, waiting for transfers between devices, body(): lax.all_gather(out_weight, ('seq', 'dp'), axis=0, tiled=True)  38.9 us
    add x31, other arithmetic, add_pair(): return earlier + latter  29.9 us
    unnamed x30, local copies, waits for them, and re-layouts  15.5 us
    unnamed x6, waiting for transfers between devices  14.6 us
  transfers between devices with their start and end apart: 5, of which 5 were waited for; matrix products, arithmetic and copies ran while one was open for 11% of the time, Pallas kernels for 0%

commit v1 on v0

v1 whole, which is shorter than its diff:
```python
import math

import jax
import jax.numpy as jnp
from jax import lax
from jax.experimental import pallas as pl
from jax.experimental.pallas import tpu as pltpu
from jax.sharding import Mesh
from jax.sharding import PartitionSpec as P

HEAD_DIM = 128
HEADS = 4
TOKENS = 512
WIDTH = 512
EPS = 1e-06
BF = jnp.bfloat16
F32 = jnp.float32
PLANE = ("y", "dp")
BLOCKS = ("y", "core", "dp")
VMEM_LIMIT = 48 * 1024 * 1024


def dot(a, b, dims):
    return lax.dot_general(a, b, (dims, ((), ())), preferred_element_type=F32)


NN = ((1,), (0,))
NT = ((1,), (1,))
TN = ((0,), (0,))


def head(ref, h):
    return ref[:, h * HEAD_DIM : (h + 1) * HEAD_DIM]


def causal_mask():
    rows = lax.broadcasted_iota(jnp.int32, (TOKENS, TOKENS), 0)
    cols = lax.broadcasted_iota(jnp.int32, (TOKENS, TOKENS), 1)
    return rows >= cols


def call(kernel, out, n_in, flops, any_in=0, scratch=()):
    vmem = pl.BlockSpec(memory_space=pltpu.VMEM)
    anys = pl.BlockSpec(memory_space=pl.ANY)
    return pl.pallas_call(
        kernel,
        out_shape=tuple(jax.ShapeDtypeStruct(s, d) for s, d in out),
        in_specs=[anys] * any_in + [vmem] * n_in,
        out_specs=tuple(vmem for _ in out),
        scratch_shapes=scratch,
        compiler_params=pltpu.CompilerParams(vmem_limit_bytes=VMEM_LIMIT),
        cost_estimate=pl.CostEstimate(flops=flops, bytes_accessed=4 << 20, transcendentals=0),
    )


def state_kernel(k_ref, v_ref, out_ref):
    for h in range(HEADS):
        state = dot(head(k_ref, h), head(v_ref, h), TN).astype(BF)
        out_ref[h * 8 : (h + 1) * 8] = state.reshape(8, 16, HEAD_DIM)


def intra_kernel(q_ref, k_ref, v_ref, att_ref):
    mask = causal_mask()
    for h in range(HEADS):
        scores = dot(head(q_ref, h), head(k_ref, h), NT)
        scores = jnp.where(mask, scores, 0.0).astype(BF)
        att_ref[:, h * HEAD_DIM : (h + 1) * HEAD_DIM] = dot(scores, head(v_ref, h), NN)


def scan_kernel(in_ref, out_ref):
    total = jnp.zeros((16, HEAD_DIM), F32)
    for c in range(32):
        out_ref[c] = total.astype(BF)
        total = total + in_ref[c].astype(F32)


def scan_back_kernel(in_ref, out_ref, gain_ref):
    total = jnp.zeros((16, HEAD_DIM), F32)
    gain = jnp.zeros((16, HEAD_DIM), F32)
    for c in range(31, -1, -1):
        out_ref[c] = total.astype(BF)
        total = total + in_ref[c, 0:16].astype(F32)
        gain = gain + in_ref[c, 16:32].astype(F32)
    gain_ref[...] = (gain[0:4] + gain[4:8]) * (1.0 / math.sqrt(16384.0))


def norm_kernel(q_ref, prior_ref, gain_ref, intra_ref, att_ref, gated_ref):
    for h in range(HEADS):
        cols = slice(h * HEAD_DIM, (h + 1) * HEAD_DIM)
        prior = prior_ref[h * 8 : (h + 1) * 8].reshape(HEAD_DIM, HEAD_DIM)
        att = intra_ref[:, cols] + dot(q_ref[:, cols], prior, NN)
        att_ref[:, cols] = att
        inverse = lax.rsqrt(jnp.mean(att * att, axis=-1, keepdims=True) + EPS)
        gated = (att * inverse * gain_ref[:, cols]).astype(BF)
        gated_ref[cols, :] = gated.T


def load_rows(chunks, a_vmem, sems):
    place = lax.axis_index("tp")
    copies = []
    for i, k in enumerate((0, 1, -1, 2, -2, 3, -3)):
        j = lax.rem(place + 8 - k, 8)
        copies.append(pltpu.make_async_copy(chunks[i], a_vmem.at[j], sems.at[i]))
    j = lax.rem(place + 4, 8)
    half = TOKENS // 2
    copies.append(pltpu.make_async_copy(chunks[7], a_vmem.at[j, 0:half], sems.at[7]))
    copies.append(pltpu.make_async_copy(chunks[8], a_vmem.at[j, half:TOKENS], sems.at[8]))
    return copies


def weight_kernel(*refs):
    chunks, (gated_ref, mine_ref, other_ref, a_vmem, sems) = refs[:9], refs[9:]
    copies = load_rows(chunks, a_vmem, sems)
    for c in copies:
        c.start()
    for c in copies:
        c.wait()
    core = lax.axis_index("core")
    for out, parity in ((mine_ref, core), (other_ref, 1 - core)):
        for y in range(4):
            part = dot(gated_ref[...], a_vmem[2 * y + parity], NN).astype(BF)
            for x in range(4):
                out[4 * y + x] = part[:, x * 128 : (x + 1) * 128]


def grad_kernel(*refs):
    chunks, rest = refs[:9], refs[9:]
    wm, wo, q_ref, att_ref, gain_ref, ga_ref, send_ref, a_vmem, w_vmem, acc, sems, wsems = rest
    core = lax.axis_index("core")
    copies = load_rows(chunks, a_vmem, sems)
    for y in range(4):
        rows = slice(4 * y, 4 * y + 4)
        copies.append(pltpu.make_async_copy(wm.at[rows], w_vmem.at[2 * y + core], wsems.at[y]))
        copies.append(
            pltpu.make_async_copy(wo.at[rows], w_vmem.at[2 * y + 1 - core], wsems.at[4 + y])
        )
    for c in copies:
        c.start()
    for c in copies:
        c.wait()
    for j in range(8):
        part = dot(a_vmem[j], w_vmem[j].reshape(WIDTH, WIDTH), NN)
        acc[...] = part if j == 0 else acc[...] + part
    for h in range(HEADS):
        cols = slice(h * HEAD_DIM, (h + 1) * HEAD_DIM)
        att = att_ref[:, cols]
        inverse = lax.rsqrt(jnp.mean(att * att, axis=-1, keepdims=True) + EPS)
        normed = att * inverse
        grad = acc[:, cols]
        gain_part = jnp.sum(grad * normed, axis=0, keepdims=True)
        grad = grad * gain_ref[:, cols]
        grad = (grad - normed * jnp.mean(grad * normed, axis=-1, keepdims=True)) * inverse
        grad = grad.astype(BF)
        ga_ref[:, cols] = grad
        state = dot(q_ref[:, cols], grad, TN).astype(BF)
        send_ref[h * 8 : (h + 1) * 8, 0:16, :] = state.reshape(8, 16, HEAD_DIM)
        high = gain_part.astype(BF).astype(F32)
        low = gain_part - high
        acc[h : h + 1, 0:HEAD_DIM] = high
        acc[4 + h : 5 + h, 0:HEAD_DIM] = low
    acc[8:16, 0:HEAD_DIM] = jnp.zeros((8, HEAD_DIM), F32)
    rows = acc[0:16, 0:HEAD_DIM].astype(BF)
    for c in range(32):
        send_ref[c, 16:32, :] = rows


def post_kernel(q_ref, k_ref, v_ref, ga_ref, prior_ref, qg_ref, kp_ref, vp_ref):
    mask = causal_mask()
    for h in range(HEADS):
        cols = slice(h * HEAD_DIM, (h + 1) * HEAD_DIM)
        q, k, v, ga = q_ref[:, cols], k_ref[:, cols], v_ref[:, cols], ga_ref[:, cols]
        prior = prior_ref[h * 8 : (h + 1) * 8].reshape(HEAD_DIM, HEAD_DIM)
        scores = jnp.where(mask, dot(q, k, NT), 0.0).astype(BF)
        vp_ref[:, cols] = dot(scores, ga, TN)
        back = jnp.where(mask, dot(ga, v, NT), 0.0).astype(BF)
        qg_ref[:, cols] = (dot(back, k, NN) + dot(ga, prior, NT)).astype(BF)
        kp_ref[:, cols] = dot(back, q, TN)


def final_kernel(k_ref, v_ref, later_ref, kp_ref, vp_ref, kg_ref, vg_ref):
    for h in range(HEADS):
        cols = slice(h * HEAD_DIM, (h + 1) * HEAD_DIM)
        later = later_ref[h * 8 : (h + 1) * 8].reshape(HEAD_DIM, HEAD_DIM)
        kg_ref[:, cols] = (kp_ref[:, cols] + dot(v_ref[:, cols], later, NT)).astype(BF)
        vg_ref[:, cols] = (vp_ref[:, cols] + dot(k_ref[:, cols], later, NN)).astype(BF)


def sum_kernel(in_ref, out_ref):
    total = in_ref[0].astype(F32)
    for c in range(1, 16):
        total = total + in_ref[c].astype(F32)
    out_ref[...] = (total * (1.0 / math.sqrt(16384.0))).T


def around(n, k):
    return [(i, (i + k) % n) for i in range(n)]


def swap_cores(x):
    return lax.ppermute(x, "core", [(0, 1), (1, 0)])


def exchange(x, axes):
    return lax.all_to_all(x, axes, 0, 0, tiled=True)


def body(queries, keys, values, gain, out_weight, out_cotangent):
    square = (TOKENS, WIDTH)
    up, down = around(8, 1), around(8, -1)
    half = TOKENS // 2
    chunks = [out_cotangent]
    fwd = bwd = out_cotangent
    for _ in range(3):
        fwd = lax.ppermute(fwd, "tp", up)
        bwd = lax.ppermute(bwd, "tp", down)
        chunks += [fwd, bwd]
    chunks += [lax.ppermute(fwd[:half], "tp", up), lax.ppermute(bwd[half:], "tp", down)]

    (state,) = call(state_kernel, [((32, 16, 128), BF)], 2, 1 << 27)(keys, values)
    states = exchange(state, BLOCKS)
    (priors,) = call(scan_kernel, [((32, 16, 128), BF)], 1, 1 << 22)(states)
    prior = exchange(priors, BLOCKS)
    (intra,) = call(intra_kernel, [(square, F32)], 3, 1 << 30)(queries, keys, values)
    w_mine = exchange(jnp.broadcast_to(out_weight[None], (16, 128, WIDTH)), PLANE)
    w_other = swap_cores(w_mine)
    gain_row = gain.reshape(1, WIDTH)
    att, gated = call(norm_kernel, [(square, F32), (square, BF)], 4, 1 << 28)(
        queries, prior, gain_row, intra
    )
    rows_scratch = [pltpu.VMEM((8, TOKENS, WIDTH), BF)]
    mine, other = call(
        weight_kernel,
        [((16, WIDTH, 128), BF), ((16, WIDTH, 128), BF)],
        1,
        1 << 32,
        9,
        rows_scratch + [pltpu.SemaphoreType.DMA((9,))],
    )(*chunks, gated)
    ga, send = call(
        grad_kernel,
        [(square, BF), ((32, 32, 128), BF)],
        3,
        1 << 32,
        11,
        rows_scratch
        + [
            pltpu.VMEM((8, 4, 128, WIDTH), BF),
            pltpu.VMEM(square, F32),
            pltpu.SemaphoreType.DMA((9,)),
            pltpu.SemaphoreType.DMA((8,)),
        ],
    )(*chunks, w_mine, w_other, queries, att, gain_row)
    received = exchange(send, BLOCKS)
    laters, gain_sum = call(scan_back_kernel, [((32, 16, 128), BF), ((4, 128), F32)], 1, 1 << 22)(
        received
    )
    later = exchange(laters, BLOCKS)
    query_grad, key_part, value_part = call(
        post_kernel, [(square, BF), (square, F32), (square, F32)], 5, 1 << 31
    )(queries, keys, values, ga, prior)
    both = (mine.astype(F32) + swap_cores(other).astype(F32)).astype(BF)
    parts = exchange(both, PLANE)
    (weight_grad,) = call(sum_kernel, [((128, WIDTH), F32)], 1, 1 << 22)(parts)
    key_grad, value_grad = call(final_kernel, [(square, BF), (square, BF)], 5, 1 << 28)(
        keys, values, later, key_part, value_part
    )
    return query_grad, key_grad, value_grad, gain_sum.reshape(WIDTH), weight_grad


def solution(mesh):
    grid = Mesh(mesh.devices.reshape(4, 2, 8, 4), ("y", "core", "tp", "dp"))
    rows = P(("y", "core", "dp"), "tp")
    return jax.shard_map(
        body,
        mesh=grid,
        in_specs=(rows, rows, rows, P("tp"), rows, rows),
        out_specs=(rows, rows, rows, P("tp"), rows),
        check_vma=False,
    )
```

time: 364 us -> 159 us (0.44)
  the two profiles are of different devices: /device:TPU:6 before, /device:TPU:1 now
where the time goes in v1:
time: 159 us; the launch traced here: 158 us
  waiting for transfers between devices  55.5 us (35%)
  starting transfers between devices  48.4 us (30%)
  Pallas kernels  23.6 us (15%)
  local copies, waits for them, and re-layouts  12.7 us (8%)
  blocking collectives  12.5 us (8%)
  other arithmetic  4.14 us (3%)
    all_to_all x5, waiting for transfers between devices, exchange(): return lax.all_to_all(x, axes, 0, 0, tiled=True)  36.8 us
    all_to_all x5, starting transfers between devices, exchange(): return lax.all_to_all(x, axes, 0, 0, tiled=True)  30.4 us
    ppermute x3, waiting for transfers between devices, body(): bwd = lax.ppermute(bwd, 'tp', down)  18.1 us
    ppermute x3, starting transfers between devices, body(): bwd = lax.ppermute(bwd, 'tp', down)  12.7 us
    all_to_all x1, blocking collectives, exchange(): return lax.all_to_all(x, axes, 0, 0, tiled=True)  12.5 us
    unnamed x36, local copies, waits for them, and re-layouts  8.82 us
    pallas_call x1, Pallas kernels, body(): call(grad_kernel, [(square, BF), ((32, 32, 128), BF)], 3, 1 << 32, 11, ro...  6.99 us
    pallas_call x1, Pallas kernels, body(): call(weight_kernel, [((16, WIDTH, 128), BF), ((16, WIDTH, 128), BF)], 1,...  5.96 us
  transfers between devices with their start and end apart: 15, of which 7 were waited for; matrix products, arithmetic and copies ran while one was open for 4% of the time, Pallas kernels for 14%

profile of v1, /device:TPU:1, one launch (start us, length us, event | category | flops | bytes accessed | tf_op | source)
XLA Modules:
  0.0 157.7 jit_solution(1640547777409990506)
XLA Ops:
  0.6 2.4 %broadcast_in_dim.2 = bf16[16,128,512]{2,1,0:T(8,128)(2,1)} broadcast(bf16[128,512]{1,0:T(8,128)(2,1)} %param.10), dimensions={1,2} | broadcast | bytes 2228224 | tf_op jit(solution)/shard_map/broadcast_in_dim | solution.py:224
  3.1 7.8 %all-to-all-start = ((bf16[16,128,512]{2,1,0:T(8,128)(2,1)}), bf16[16,128,512]{2,1,0:T(8,128)(2,1)}, u32[]{:S(2)}, u32[]{:S(2)}) async-start(bf16[16,128,512]{2,1,0:T(8,128)(2,1)} %broadcast_in_dim.2), calls=%async_computation | async-start | bytes 4194304 | tf_op jit(solution)/shard_map/all_to_all | solution.py:204
  10.9 5.7 %collective-permute-start.1 = (bf16[512,512]{1,0:T(8,128)(2,1)S(1)}, bf16[512,512]{1,0:T(8,128)(2,1)S(1)}, u32[]{:S(2)}, u32[]{:S(2)}) collective-permute-start(bf16[512,512]{1,0:T(8,128)(2,1)S(1)} %copy-done.9), channel_id=1, source_target_pairs={{0,28},{4,0},{8,4},{12,8},{16,12},{20,16},{24,20},{28,24},{1,29},{... | collective-permute-start | bytes 1572872 | tf_op jit(solution)/shard_map/ppermute | solution.py:215
  16.5 10.3 %collective-permute-done.1.refs_2_ = bf16[512,512]{1,0:T(8,128)(2,1)S(1)} collective-permute-done((bf16[512,512]{1,0:T(8,128)(2,1)S(1)}, bf16[512,512]{1,0:T(8,128)(2,1)S(1)}, u32[]{:S(2)}, u32[]{:S(2)}) %collective-permute-start.1) | collective-permute-done | bytes 524320 | tf_op jit(solution)/shard_map/ppermute | solution.py:215
  26.8 3.5 %collective-permute-start.3 = (bf16[512,512]{1,0:T(8,128)(2,1)S(1)}, bf16[512,512]{1,0:T(8,128)(2,1)}, u32[]{:S(2)}, u32[]{:S(2)}) collective-permute-start(bf16[512,512]{1,0:T(8,128)(2,1)S(1)} %collective-permute-done.1.refs_2_), channel_id=1, source_target_pairs={{0,28},{4,0},{8,4},{12,8},{16,12},{20,16},{24,20},{28,24},{1,29},{... | collective-permute-start | bytes 1572872 | tf_op jit(solution)/shard_map/ppermute | solution.py:215
  31.9 7.9 %collective-permute-done.3.refs_4_ = bf16[512,512]{1,0:T(8,128)(2,1)} collective-permute-done((bf16[512,512]{1,0:T(8,128)(2,1)S(1)}, bf16[512,512]{1,0:T(8,128)(2,1)}, u32[]{:S(2)}, u32[]{:S(2)}) %collective-permute-start.3) | collective-permute-done | bytes 524320 | tf_op jit(solution)/shard_map/ppermute | solution.py:215
  39.8 3.5 %collective-permute-start.5 = (bf16[512,512]{1,0:T(8,128)(2,1)}, bf16[512,512]{1,0:T(8,128)(2,1)S(1)}, u32[]{:S(2)}, u32[]{:S(2)}) collective-permute-start(bf16[512,512]{1,0:T(8,128)(2,1)} %collective-permute-done.3.refs_4_), channel_id=1, source_target_pairs={{0,28},{4,0},{8,4},{12,8},{16,12},{20,16},{24,20},{28,24},{1,29},{... | collective-permute-start | bytes 1572872 | tf_op jit(solution)/shard_map/ppermute | solution.py:215
  44.8 9.5 %all-to-all-start.1 = ((bf16[32,16,128]{2,1,0:T(8,128)(2,1)}), bf16[32,16,128]{2,1,0:T(8,128)(2,1)S(1)}, u32[]{:S(2)}, u32[]{:S(2)}) async-start(bf16[32,16,128]{2,1,0:T(8,128)(2,1)} %shard_map.101), calls=%async_computation.1 | async-start | bytes 262144 | tf_op jit(solution)/shard_map/all_to_all | solution.py:204
  55.1 2.9 %collective-permute-start.7 = (bf16[256,512]{1,0:T(8,128)(2,1)}, bf16[256,512]{1,0:T(8,128)(2,1)}, u32[]{:S(2)}, u32[]{:S(2)}) collective-permute-start(bf16[256,512]{1,0:T(8,128)(2,1)} %slice.9), channel_id=1, source_target_pairs={{0,28},{4,0},{8,4},{12,8},{16,12},{20,16},{24,20},{28,24},{1,29},{... | collective-permute-start | bytes 786440 | tf_op jit(solution)/shard_map/ppermute | solution.py:217
  58.8 2.0 %collective-permute-start.8 = (bf16[16,128,512]{2,1,0:T(8,128)(2,1)}, bf16[16,128,512]{2,1,0:T(8,128)(2,1)}, u32[]{:S(2)}, u32[]{:S(2)}) collective-permute-start(bf16[16,128,512]{2,1,0:T(8,128)(2,1)} %all-to-all-done.refs_9_), channel_id=1, source_target_pairs={{0,32},{32,0},{1,33},{33,1},{2,34},{34,2},{3,35},{35,3},{4,36},{36... | collective-permute-start | bytes 6291464 | tf_op jit(solution)/shard_map/ppermute | solution.py:200
  60.8 1.1 all-to-all-done.1.in_ref
  62.7 5.3 %all-to-all-start.2 = ((bf16[32,16,128]{2,1,0:T(8,128)(2,1)}), bf16[32,16,128]{2,1,0:T(8,128)(2,1)S(1)}, u32[]{:S(2)}, u32[]{:S(2)}) async-start(bf16[32,16,128]{2,1,0:T(8,128)(2,1)} %shard_map.102), calls=%async_computation.2 | async-start | bytes 262144 | tf_op jit(solution)/shard_map/all_to_all | solution.py:204
  67.9 1.3 shard_map.103.intra_ref
  69.3 6.2 %all-to-all-done.2.prior_ref = bf16[32,16,128]{2,1,0:T(8,128)(2,1)S(1)} async-done(((bf16[32,16,128]{2,1,0:T(8,128)(2,1)}), bf16[32,16,128]{2,1,0:T(8,128)(2,1)S(1)}, u32[]{:S(2)}, u32[]{:S(2)}) %all-to-all-start.2) | async-done | bytes 131104 | tf_op jit(solution)/shard_map/all_to_all | solution.py:204
  81.3 6.0 %shard_map.109 = (bf16[16,512,128]{2,1,0:T(8,128)(2,1)}, bf16[16,512,128]{2,1,0:T(8,128)(2,1)}) custom-call(bf16[512,512]{1,0:T(8,128)(2,1)S(1)} %copy-done.10, bf16[512,512]{1,0:T(8,128)(2,1)S(1)} %copy-done.15, bf16[512,512]{1,0:T(8,128)(2,1)S(1)} %copy-done.12, bf16[512,512]{1,0:T(8,128)(2,1)} %collective-permute-done.2.refs_3_, ...), custom_call_target="tpu_custom_call" | custom-call | flops 4294967296 | bytes 4194304 | tf_op jit(solution)/shard_map/pallas_call | solution.py:231
  87.7 7.0 %shard_map.105 = (bf16[512,512]{1,0:T(8,128)(2,1)S(1)}, bf16[32,32,128]{2,1,0:T(8,128)(2,1)S(1)}) custom-call(bf16[512,512]{1,0:T(8,128)(2,1)S(1)} %copy-done.10, bf16[512,512]{1,0:T(8,128)(2,1)S(1)} %copy-done.15, bf16[512,512]{1,0:T(8,128)(2,1)S(1)} %copy-done.13, bf16[512,512]{1,0:T(8,128)(2,1)} %collective-permute-done.2.refs_3_, ...), custom_call_target="tpu_custom_call" | custom-call | flops 4294967296 | bytes 4194304 | tf_op jit(solution)/shard_map/pallas_call | solution.py:239
  94.7 12.5 %all_to_all.30.in_ref = bf16[32,32,128]{2,1,0:T(8,128)(2,1)S(1)} all-to-all(bf16[32,32,128]{2,1,0:T(8,128)(2,1)S(1)} %get-tuple-element.21), channel_id=1, replica_groups=mesh['y'=4,'core'=2,'tp'=8,'dp'=4] {'y','core','dp'}, dimensions={0} | all-to-all | bytes 524288 | tf_op jit(solution)/shard_map/all_to_all | solution.py:204
  107.9 4.1 %all-to-all-start.4 = ((bf16[32,16,128]{2,1,0:T(8,128)(2,1)}), bf16[32,16,128]{2,1,0:T(8,128)(2,1)S(1)}, u32[]{:S(2)}, u32[]{:S(2)}) async-start(bf16[32,16,128]{2,1,0:T(8,128)(2,1)} %get-tuple-element.22), calls=%async_computation.4 | async-start | bytes 262144 | tf_op jit(solution)/shard_map/all_to_all | solution.py:204
  112.1 4.1 %add_convert_fusion = bf16[16,512,128]{2,1,0:T(8,128)(2,1)} fusion(bf16[16,512,128]{2,1,0:T(8,128)(2,1)} %collective-permute-done.9, bf16[16,512,128]{2,1,0:T(8,128)(2,1)} %get-tuple-element.29), kind=kLoop, calls=%fused_computation | loop fusion | flops 4194304 | bytes 6291456 | tf_op jit(solution)/shard_map/convert_element_type | solution.py:261
  116.2 3.5 %all-to-all-done.4.later_ref = bf16[32,16,128]{2,1,0:T(8,128)(2,1)S(1)} async-done(((bf16[32,16,128]{2,1,0:T(8,128)(2,1)}), bf16[32,16,128]{2,1,0:T(8,128)(2,1)S(1)}, u32[]{:S(2)}, u32[]{:S(2)}) %all-to-all-start.4) | async-done | bytes 131104 | tf_op jit(solution)/shard_map/all_to_all | solution.py:204
  119.7 3.7 %all-to-all-start.5 = ((bf16[16,512,128]{2,1,0:T(8,128)(2,1)}), bf16[16,512,128]{2,1,0:T(8,128)(2,1)S(1)}, u32[]{:S(2)}, u32[]{:S(2)}) async-start(bf16[16,512,128]{2,1,0:T(8,128)(2,1)} %add_convert_fusion), calls=%async_computation.5 | async-start | bytes 4194304 | tf_op jit(solution)/shard_map/all_to_all | solution.py:204
  125.5 3.8 %shard_map.106 = (bf16[512,512]{1,0:T(8,128)(2,1)}, f32[512,512]{1,0:T(8,128)S(1)}, f32[512,512]{1,0:T(8,128)S(1)}) custom-call(bf16[512,512]{1,0:T(8,128)(2,1)S(1)} %copy-done.3, bf16[512,512]{1,0:T(8,128)(2,1)S(1)} %copy-done, bf16[512,512]{1,0:T(8,128)(2,1)S(1)} %copy-done.1, bf16[512,512]{1,0:T(8,128)(2,1)S(1)} %copy-done.17, ...), custom_call_target="tpu_custom_call" | custom-call | flops 2147483648 | bytes 4194304 | tf_op jit(solution)/shard_map/pallas_call | solution.py:258
  129.3 1.4 shard_map.108
  130.7 26.0 %all-to-all-done.5.in_ref = bf16[16,512,128]{2,1,0:T(8,128)(2,1)S(1)} async-done(((bf16[16,512,128]{2,1,0:T(8,128)(2,1)}), bf16[16,512,128]{2,1,0:T(8,128)(2,1)S(1)}, u32[]{:S(2)}, u32[]{:S(2)}) %all-to-all-start.5) | async-done | bytes 2097184 | tf_op jit(solution)/shard_map/all_to_all | solution.py:204
  (57 shorter events, 15.3 us)
Async XLA Ops:
  3.1 7.8 %copy-start.9 = (bf16[512,512]{1,0:T(8,128)(2,1)S(1)}, bf16[512,512]{1,0:T(8,128)(2,1)}, u32[]{:S(2)}) copy-start(bf16[512,512]{1,0:T(8,128)(2,1)} %refs_0_.3) | copy-start | bytes 1572868
  3.1 40.7 %copy-start = (bf16[512,512]{1,0:T(8,128)(2,1)S(1)}, bf16[512,512]{1,0:T(8,128)(2,1)}, u32[]{:S(2)}) copy-start(bf16[512,512]{1,0:T(8,128)(2,1)} %k_ref.7) | copy-start | bytes 1572868
  3.1 40.7 %copy-start.1 = (bf16[512,512]{1,0:T(8,128)(2,1)S(1)}, bf16[512,512]{1,0:T(8,128)(2,1)}, u32[]{:S(2)}) copy-start(bf16[512,512]{1,0:T(8,128)(2,1)} %v_ref.7) | copy-start | bytes 1572868
  3.1 41.8 %all-to-all-start = ((bf16[16,128,512]{2,1,0:T(8,128)(2,1)}), bf16[16,128,512]{2,1,0:T(8,128)(2,1)}, u32[]{:S(2)}, u32[]{:S(2)}) async-start(bf16[16,128,512]{2,1,0:T(8,128)(2,1)} %broadcast_in_dim.2), calls=%async_computation | async-start | bytes 4194304 | tf_op jit(solution)/shard_map/all_to_all | solution.py:204
  10.9 57.1 %copy-start.2 = (bf16[512,512]{1,0:T(8,128)(2,1)S(1)}, bf16[512,512]{1,0:T(8,128)(2,1)}, u32[]{:S(2)}) copy-start(bf16[512,512]{1,0:T(8,128)(2,1)} %q_ref.5) | copy-start | bytes 1572868
  10.9 15.9 %collective-permute-start.1 = (bf16[512,512]{1,0:T(8,128)(2,1)S(1)}, bf16[512,512]{1,0:T(8,128)(2,1)S(1)}, u32[]{:S(2)}, u32[]{:S(2)}) collective-permute-start(bf16[512,512]{1,0:T(8,128)(2,1)S(1)} %copy-done.9), channel_id=1, source_target_pairs={{0,28},{4,0},{8,4},{12,8},{16,12},{20,16},{24,20},{28,24},{1,29},{... | collective-permute-start | bytes 1572872 | tf_op jit(solution)/shard_map/ppermute | solution.py:215
  16.5 14.6 %collective-permute-start = (bf16[512,512]{1,0:T(8,128)(2,1)S(1)}, bf16[512,512]{1,0:T(8,128)(2,1)S(1)}, u32[]{:S(2)}, u32[]{:S(2)}) collective-permute-start(bf16[512,512]{1,0:T(8,128)(2,1)S(1)} %copy-done.9), channel_id=1, source_target_pairs={{0,4},{4,8},{8,12},{12,16},{16,20},{20,24},{24,28},{28,0},{1,5},{5... | collective-permute-start | bytes 1572872 | tf_op jit(solution)/shard_map/ppermute | solution.py:214
  26.8 13.0 %collective-permute-start.3 = (bf16[512,512]{1,0:T(8,128)(2,1)S(1)}, bf16[512,512]{1,0:T(8,128)(2,1)}, u32[]{:S(2)}, u32[]{:S(2)}) collective-permute-start(bf16[512,512]{1,0:T(8,128)(2,1)S(1)} %collective-permute-done.1.refs_2_), channel_id=1, source_target_pairs={{0,28},{4,0},{8,4},{12,8},{16,12},{20,16},{24,20},{28,24},{1,29},{... | collective-permute-start | bytes 1572872 | tf_op jit(solution)/shard_map/ppermute | solution.py:215
  31.1 12.7 %collective-permute-start.2 = (bf16[512,512]{1,0:T(8,128)(2,1)S(1)}, bf16[512,512]{1,0:T(8,128)(2,1)}, u32[]{:S(2)}, u32[]{:S(2)}) collective-permute-start(bf16[512,512]{1,0:T(8,128)(2,1)S(1)} %collective-permute-done.refs_1_), channel_id=1, source_target_pairs={{0,4},{4,8},{8,12},{12,16},{16,20},{20,24},{24,28},{28,0},{1,5},{5... | collective-permute-start | bytes 1572872 | tf_op jit(solution)/shard_map/ppermute | solution.py:214
  39.8 14.6 %collective-permute-start.5 = (bf16[512,512]{1,0:T(8,128)(2,1)}, bf16[512,512]{1,0:T(8,128)(2,1)S(1)}, u32[]{:S(2)}, u32[]{:S(2)}) collective-permute-start(bf16[512,512]{1,0:T(8,128)(2,1)} %collective-permute-done.3.refs_4_), channel_id=1, source_target_pairs={{0,28},{4,0},{8,4},{12,8},{16,12},{20,16},{24,20},{28,24},{1,29},{... | collective-permute-start | bytes 1572872 | tf_op jit(solution)/shard_map/ppermute | solution.py:215
  43.8 14.2 %collective-permute-start.4 = (bf16[512,512]{1,0:T(8,128)(2,1)}, bf16[512,512]{1,0:T(8,128)(2,1)S(1)}, u32[]{:S(2)}, u32[]{:S(2)}) collective-permute-start(bf16[512,512]{1,0:T(8,128)(2,1)} %collective-permute-done.2.refs_3_), channel_id=1, source_target_pairs={{0,4},{4,8},{8,12},{12,16},{16,20},{20,24},{24,28},{28,0},{1,5},{5... | collective-permute-start | bytes 1572872 | tf_op jit(solution)/shard_map/ppermute | solution.py:214
  44.8 17.1 %all-to-all-start.1 = ((bf16[32,16,128]{2,1,0:T(8,128)(2,1)}), bf16[32,16,128]{2,1,0:T(8,128)(2,1)S(1)}, u32[]{:S(2)}, u32[]{:S(2)}) async-start(bf16[32,16,128]{2,1,0:T(8,128)(2,1)} %shard_map.101), calls=%async_computation.1 | async-start | bytes 262144 | tf_op jit(solution)/shard_map/all_to_all | solution.py:204
  55.1 22.1 %collective-permute-start.7 = (bf16[256,512]{1,0:T(8,128)(2,1)}, bf16[256,512]{1,0:T(8,128)(2,1)}, u32[]{:S(2)}, u32[]{:S(2)}) collective-permute-start(bf16[256,512]{1,0:T(8,128)(2,1)} %slice.9), channel_id=1, source_target_pairs={{0,28},{4,0},{8,4},{12,8},{16,12},{20,16},{24,20},{28,24},{1,29},{... | collective-permute-start | bytes 786440 | tf_op jit(solution)/shard_map/ppermute | solution.py:217
  58.0 4.6 %copy-start.4 = (bf16[512,512]{1,0:T(8,128)(2,1)}, bf16[512,512]{1,0:T(8,128)(2,1)S(1)}, u32[]{:S(2)}) copy-start(bf16[512,512]{1,0:T(8,128)(2,1)S(1)} %collective-permute-done.4.refs_5_) | copy-start | bytes 1572868
  58.8 18.4 %collective-permute-start.6 = (bf16[256,512]{1,0:T(8,128)(2,1)}, bf16[256,512]{1,0:T(8,128)(2,1)}, u32[]{:S(2)}, u32[]{:S(2)}) collective-permute-start(bf16[256,512]{1,0:T(8,128)(2,1)} %slice.8), channel_id=1, source_target_pairs={{0,4},{4,8},{8,12},{12,16},{16,20},{20,24},{24,28},{28,0},{1,5},{5... | collective-permute-start | bytes 786440 | tf_op jit(solution)/shard_map/ppermute | solution.py:217
  58.8 28.9 %collective-permute-start.8 = (bf16[16,128,512]{2,1,0:T(8,128)(2,1)}, bf16[16,128,512]{2,1,0:T(8,128)(2,1)}, u32[]{:S(2)}, u32[]{:S(2)}) collective-permute-start(bf16[16,128,512]{2,1,0:T(8,128)(2,1)} %all-to-all-done.refs_9_), channel_id=1, source_target_pairs={{0,32},{32,0},{1,33},{33,1},{2,34},{34,2},{3,35},{35,3},{4,36},{36... | collective-permute-start | bytes 6291464 | tf_op jit(solution)/shard_map/ppermute | solution.py:200
  62.7 12.9 %copy-start.7 = (f32[512]{0:T(512)S(1)}, f32[512]{0:T(512)}, u32[]{:S(2)}) copy-start(f32[512]{0:T(512)} %param.9) | copy-start | bytes 6148
  62.7 12.9 %all-to-all-start.2 = ((bf16[32,16,128]{2,1,0:T(8,128)(2,1)}), bf16[32,16,128]{2,1,0:T(8,128)(2,1)S(1)}, u32[]{:S(2)}, u32[]{:S(2)}) async-start(bf16[32,16,128]{2,1,0:T(8,128)(2,1)} %shard_map.102), calls=%async_computation.2 | async-start | bytes 262144 | tf_op jit(solution)/shard_map/all_to_all | solution.py:204
  81.3 6.4 %copy-start.6 = (bf16[512,512]{1,0:T(8,128)(2,1)S(1)}, bf16[512,512]{1,0:T(8,128)(2,1)}, u32[]{:S(2)}) copy-start(bf16[512,512]{1,0:T(8,128)(2,1)} %copy-done.4) | copy-start | bytes 1572868
  81.3 6.4 %copy-start.13 = (bf16[512,512]{1,0:T(8,128)(2,1)S(1)}, bf16[512,512]{1,0:T(8,128)(2,1)}, u32[]{:S(2)}) copy-start(bf16[512,512]{1,0:T(8,128)(2,1)} %copy-done.11) | copy-start | bytes 1572868
  87.3 24.8 %collective-permute-start.9 = (bf16[16,512,128]{2,1,0:T(8,128)(2,1)}, bf16[16,512,128]{2,1,0:T(8,128)(2,1)}, u32[]{:S(2)}, u32[]{:S(2)}) collective-permute-start(bf16[16,512,128]{2,1,0:T(8,128)(2,1)} %get-tuple-element.30), channel_id=1, source_target_pairs={{0,32},{32,0},{1,33},{33,1},{2,34},{34,2},{3,35},{35,3},{4,36},{36... | collective-permute-start | bytes 6291464 | tf_op jit(solution)/shard_map/ppermute | solution.py:200
  94.7 13.2 %copy-start.16 = (bf16[512,512]{1,0:T(8,128)(2,1)}, bf16[512,512]{1,0:T(8,128)(2,1)S(1)}, u32[]{:S(2)}) copy-start(bf16[512,512]{1,0:T(8,128)(2,1)S(1)} %get-tuple-element.19.ga_ref) | copy-start | bytes 1572868
  107.9 11.7 %all-to-all-start.4 = ((bf16[32,16,128]{2,1,0:T(8,128)(2,1)}), bf16[32,16,128]{2,1,0:T(8,128)(2,1)S(1)}, u32[]{:S(2)}, u32[]{:S(2)}) async-start(bf16[32,16,128]{2,1,0:T(8,128)(2,1)} %get-tuple-element.22), calls=%async_computation.4 | async-start | bytes 262144 | tf_op jit(solution)/shard_map/all_to_all | solution.py:204
  119.7 37.0 %all-to-all-start.5 = ((bf16[16,512,128]{2,1,0:T(8,128)(2,1)}), bf16[16,512,128]{2,1,0:T(8,128)(2,1)S(1)}, u32[]{:S(2)}, u32[]{:S(2)}) async-start(bf16[16,512,128]{2,1,0:T(8,128)(2,1)} %add_convert_fusion), calls=%async_computation.5 | async-start | bytes 4194304 | tf_op jit(solution)/shard_map/all_to_all | solution.py:204
  (9 other events, 8.8 us)

commit v2 on v0

v2 whole, which is shorter than its diff:
```python
import math

import jax
import jax.numpy as jnp
from jax import lax
from jax.experimental import pallas as pl
from jax.experimental.pallas import tpu as pltpu
from jax.sharding import Mesh
from jax.sharding import PartitionSpec as P

HEAD_DIM = 128
HEADS = 4
TOKENS = 512
WIDTH = 512
RING = 8
EPS = 1e-06
SCALE = 1.0 / math.sqrt(16384.0)
BF = jnp.bfloat16
F32 = jnp.float32
PLANE = ("y", "dp")
VMEM_LIMIT = 24 * 1024 * 1024
STATE = (HEADS * HEAD_DIM, HEAD_DIM)
STATE_GAIN = (HEADS * HEAD_DIM + 16, HEAD_DIM)
SQUARE = (TOKENS, WIDTH)

NN = ((1,), (0,))
NT = ((1,), (1,))
TN = ((0,), (0,))


def dot(a, b, dims):
    return lax.dot_general(a, b, (dims, ((), ())), preferred_element_type=F32)


def span(h):
    return slice(h * HEAD_DIM, (h + 1) * HEAD_DIM)


def causal_mask():
    rows = lax.broadcasted_iota(jnp.int32, (TOKENS, TOKENS), 0)
    cols = lax.broadcasted_iota(jnp.int32, (TOKENS, TOKENS), 1)
    return rows >= cols


def call(kernel, out, n_in, flops, any_in=0, scratch=(), any_out=False):
    vmem = pl.BlockSpec(memory_space=pltpu.VMEM)
    anys = pl.BlockSpec(memory_space=pl.ANY)
    return pl.pallas_call(
        kernel,
        out_shape=tuple(jax.ShapeDtypeStruct(s, d) for s, d in out),
        in_specs=[anys] * any_in + [vmem] * n_in,
        out_specs=tuple(anys if any_out else vmem for _ in out),
        scratch_shapes=scratch,
        compiler_params=pltpu.CompilerParams(vmem_limit_bytes=VMEM_LIMIT),
        cost_estimate=pl.CostEstimate(flops=flops, bytes_accessed=4 << 20, transcendentals=0),
    )


def state_kernel(k_ref, v_ref, w_ref, out_ref):
    for c in range(16):
        out_ref[c, 0:128] = w_ref[...]
        out_ref[c, 128:144, 256:] = jnp.zeros((16, 256), BF)
    for h in range(HEADS):
        state = dot(k_ref[:, span(h)], v_ref[:, span(h)], TN).astype(BF)
        for c in range(4):
            out_ref[4 * h + c, 128:144, 0:128] = state[32 * c : 32 * c + 16]
            out_ref[4 * h + c, 128:144, 128:256] = state[32 * c + 16 : 32 * c + 32]


def pick_kernel(in_ref, out_ref, part, sem):
    copy = pltpu.make_async_copy(in_ref.at[:, 128:144, 0:256], part, sem)
    copy.start()
    copy.wait()
    for c in range(16):
        out_ref[c, 0:16] = part[c, :, 0:128]
        out_ref[c, 16:32] = part[c, :, 128:256]


def scan_kernel(own_ref, other_ref, out_ref):
    second = when(lax.axis_index("core") == 1)
    run = jnp.zeros((32, HEAD_DIM), F32)
    for y in range(4):
        own = [own_ref[4 * y + x].astype(F32) for x in range(4)]
        others = sum(other_ref[4 * y + x].astype(F32) for x in range(4))
        before = run + others * second
        for x in range(4):
            out_ref[4 * y + x] = before.astype(BF)
            before = before + own[x]
        run = run + others + (own[0] + own[1] + own[2] + own[3])


def intra_kernel(q_ref, k_ref, v_ref, att_ref):
    mask = causal_mask()
    for h in range(HEADS):
        scores = dot(q_ref[:, span(h)], k_ref[:, span(h)], NT)
        scores = jnp.where(mask, scores, 0.0).astype(BF)
        att_ref[:, span(h)] = dot(scores, v_ref[:, span(h)], NN)


def when(flag):
    return jnp.where(flag, 1.0, 0.0).astype(F32)


def norm_kernel(q_ref, gain_ref, intra_ref, prior_ref, att_ref, gated_ref):
    for h in range(HEADS):
        rows = span(h)
        prior = prior_ref[rows]
        att = intra_ref[:, rows] + dot(q_ref[:, rows], prior, NN)
        att_ref[:, rows] = att
        inverse = lax.rsqrt(jnp.mean(att * att, axis=-1, keepdims=True) + EPS)
        gated = (att * inverse * gain_ref[:, rows]).astype(BF)
        gated_ref[rows, :] = gated.T


def halves(chunks):
    own, mate, f1, b1, f2, b2, f3, b3, f4, b4 = chunks

    def split(ref, k):
        return (ref.at[0:TOKENS], ref.at[TOKENS : 2 * TOKENS], k)

    same = [(own, mate, 0), split(f2, -2), split(b2, 2), (f4, b4, 4)]
    return same, [split(f1, -1), split(b1, 1), split(f3, -3), split(b3, 3)]


def by_parity(work, chunks):
    same = lax.rem(lax.axis_index("tp"), 2) == lax.axis_index("core")
    first, second = halves(chunks)
    pl.when(same)(lambda: work(first))
    pl.when(jnp.logical_not(same))(lambda: work(second))


def row_of(k):
    return lax.div(lax.rem(lax.axis_index("tp") + k + RING, RING), 2)


def main_kernel(*refs):
    chunks, rest = refs[:10], refs[10:]
    gated_ref, mate_ref, w_ref, near_ref, far_ref = rest[:5]
    own_ref, up_ref, down_ref, low_ref, high_ref, part_ref, acc = rest[5:]
    place = lax.axis_index("dp")

    def work(slots):
        for n, (near, far, k) in enumerate(slots):
            y = row_of(k)
            part = dot(gated_ref[...], near[...], NN) + dot(mate_ref[...], far[...], NN)
            part_ref[...] = part.astype(BF)
            blocks = []
            for d in range(4):
                start = pl.multiple_of(lax.rem(place + d, 4) * 128, 128)
                blocks.append(part_ref[:, pl.ds(start, 128)])
            own_ref[y], up_ref[y], down_ref[y] = blocks[0], blocks[1], blocks[3]
            low_ref[y], high_ref[y] = blocks[2][0:256], blocks[2][256:512]
            weight = w_ref[pl.ds(4 * y, 4), 0:128, :].reshape(WIDTH, WIDTH)
            part = dot(far[...], weight, NN)
            if n == 0:
                acc[...] = part
            elif n < 3:
                acc[...] += part
            else:
                far_ref[...] = (acc[...] + part).astype(BF)
            part = dot(near[...], weight, NN)
            near_ref[...] = part if n == 0 else near_ref[...] + part

    by_parity(work, chunks)


def tie(values, deps):
    def kernel(*refs):
        pass

    n = len(values)
    anys = pl.BlockSpec(memory_space=pl.ANY)
    return pl.pallas_call(
        kernel,
        out_shape=tuple(jax.ShapeDtypeStruct(v.shape, v.dtype) for v in values),
        in_specs=[anys] * (n + len(deps)),
        out_specs=(anys,) * n,
        input_output_aliases={i: i for i in range(n)},
        cost_estimate=pl.CostEstimate(flops=0, bytes_accessed=0, transcendentals=0),
    )(*values, *deps)


def relay_kernel(up_ref, down_ref, low_ref, high_ref, up_out, down_out):
    for y in range(4):
        up_out[y, 0:256] = (up_ref[y, 0:256].astype(F32) + low_ref[y].astype(F32)).astype(BF)
        up_out[y, 256:512] = up_ref[y, 256:512]
        down_out[y, 0:256] = down_ref[y, 0:256]
        low = down_ref[y, 256:512].astype(F32) + high_ref[y].astype(F32)
        down_out[y, 256:512] = low.astype(BF)


def column_kernel(own_ref, a_ref, b_ref, own_out, up_out, far_out, down_out):
    for e, out in enumerate((own_out, up_out, far_out, down_out)):
        y = lax.rem(lax.axis_index("y") + e, 4)
        total = own_ref[y].astype(F32) + a_ref[y].astype(F32) + b_ref[y].astype(F32)
        out[...] = total.astype(out.dtype)


def grad_kernel(own_ref, mate_ref, q_ref, att_ref, gain_ref, ga_ref, send_ref):
    base = HEADS * HEAD_DIM
    rows = lax.broadcasted_iota(jnp.int32, (16, HEAD_DIM), 0)
    sums = jnp.zeros((16, HEAD_DIM), F32)
    for h in range(HEADS):
        att = att_ref[:, span(h)]
        inverse = lax.rsqrt(jnp.mean(att * att, axis=-1, keepdims=True) + EPS)
        normed = att * inverse
        grad = own_ref[:, span(h)] + mate_ref[:, span(h)].astype(F32)
        part = jnp.sum(grad * normed, axis=0, keepdims=True)
        high = part.astype(BF).astype(F32)
        sums = sums + jnp.where(rows == h, high, 0.0) + jnp.where(rows == 4 + h, part - high, 0.0)
        grad = grad * gain_ref[:, span(h)]
        grad = (grad - normed * jnp.mean(grad * normed, axis=-1, keepdims=True)) * inverse
        grad = grad.astype(BF)
        ga_ref[:, span(h)] = grad
        send_ref[span(h)] = dot(q_ref[:, span(h)], grad, TN).astype(BF)
    send_ref[base:] = sums.astype(BF)


def resum(parts):
    total = sum(p.astype(F32) for p in parts)
    gain = total[0:4] + total[4:8]
    high = gain.astype(BF).astype(F32)
    return jnp.concatenate([high, gain - high, jnp.zeros((8, HEAD_DIM), F32)], axis=0)


def row_back_kernel(own_ref, r1_ref, r2_ref, r3_ref, total_ref, after_ref):
    x = lax.axis_index("dp")
    base = HEADS * HEAD_DIM
    r1, r2, r3 = (r[0:base].astype(F32) for r in (r1_ref, r2_ref, r3_ref))
    after_ref[...] = r1 * when(x <= 2) + r2 * when(x <= 1) + r3 * when(x <= 0)
    total_ref[0:base] = (own_ref[0:base].astype(F32) + r1 + r2 + r3).astype(BF)
    total_ref[base:] = resum([r[base:] for r in (own_ref, r1_ref, r2_ref, r3_ref)]).astype(BF)


def pair_back_kernel(total_ref, other_ref, out_ref):
    base = HEADS * HEAD_DIM
    out_ref[0:base] = (total_ref[0:base].astype(F32) + other_ref[0:base].astype(F32)).astype(BF)
    out_ref[base:] = resum([total_ref[base:], other_ref[base:]]).astype(BF)


def post_kernel(q_ref, k_ref, v_ref, ga_ref, prior_ref, qg_ref, kp_ref, vp_ref):
    mask = causal_mask()
    for h in range(HEADS):
        cols = span(h)
        q, k, v, ga = q_ref[:, cols], k_ref[:, cols], v_ref[:, cols], ga_ref[:, cols]
        scores = jnp.where(mask, dot(q, k, NT), 0.0).astype(BF)
        vp_ref[:, cols] = dot(scores, ga, TN)
        back = jnp.where(mask, dot(ga, v, NT), 0.0).astype(BF)
        qg_ref[:, cols] = (dot(back, k, NN) + dot(ga, prior_ref[cols], NT)).astype(BF)
        kp_ref[:, cols] = dot(back, q, TN)


def final_kernel(
    k_ref, v_ref, kp_ref, vp_ref, after_ref, other_ref, own, u1, u2, u3, kg_ref, vg_ref, gain_ref
):
    base = HEADS * HEAD_DIM
    y = lax.axis_index("y")
    first = when(lax.axis_index("core") == 0)
    for h in range(HEADS):
        cols = span(h)
        later = after_ref[cols] + other_ref[cols].astype(F32) * first
        later = later + u1[cols].astype(F32) * when(y <= 2) + u2[cols].astype(F32) * when(y <= 1)
        later = (later + u3[cols].astype(F32) * when(y <= 0)).astype(BF)
        kg_ref[:, cols] = (kp_ref[:, cols] + dot(v_ref[:, cols], later, NT)).astype(BF)
        vg_ref[:, cols] = (vp_ref[:, cols] + dot(k_ref[:, cols], later, NN)).astype(BF)
    gain_ref[...] = resum([r[base:] for r in (own, u1, u2, u3)]) * SCALE


def sum_kernel(own_ref, r1_ref, r2_ref, r3_ref, out_ref):
    total = own_ref[...]
    for ref in (r1_ref, r2_ref, r3_ref):
        total = total + ref[...].astype(F32)
    out_ref[...] = (total * SCALE).T


def shift(x, axis, size, k, wrap=True):
    pairs = [(i, (i + k) % size) for i in range(size) if wrap or 0 <= i + k < size]
    return lax.ppermute(x, axis, pairs)


def swap_cores(x):
    return lax.ppermute(x, "core", [(0, 1), (1, 0)])


def ring_step(x, parity, k):
    pairs = []
    for z in range(RING):
        core = (z + parity) % 2
        pairs.append((core * RING + z, core * RING + (z + k) % RING))
    return lax.ppermute(x, ("core", "tp"), pairs)


def body(queries, keys, values, gain, out_weight, out_cotangent):
    own = out_cotangent
    pairs = [((1 - z % 2) * RING + z, (z % 2) * RING + z) for z in range(RING)]
    mate = lax.ppermute(own, ("core", "tp"), pairs)
    chunks = [own, mate]
    fwd = bwd = jnp.concatenate([own, mate], axis=0)
    for step in range(2):
        fwd, bwd = ring_step(fwd, step, 1), ring_step(bwd, step, -1)
        chunks += [fwd, bwd]

    (spread,) = call(state_kernel, [((16, 144, WIDTH), BF)], 3, 1 << 27)(keys, values, out_weight)
    weight = lax.all_to_all(spread, PLANE, 0, 0, tiled=True)
    slices = ((16, 32, HEAD_DIM), BF)
    (states,) = call(
        pick_kernel,
        [slices],
        0,
        1 << 20,
        1,
        [pltpu.VMEM((16, 16, 256), BF), pltpu.SemaphoreType.DMA],
    )(weight)
    fwd, bwd = tie((fwd, bwd), (states,))
    chunks[4:6] = [fwd, bwd]
    fwd, bwd = ring_step(fwd, 0, 1), ring_step(bwd, 0, -1)
    chunks += [fwd, bwd, ring_step(fwd[:TOKENS], 1, 1), ring_step(bwd[TOKENS:], 1, -1)]
    (priors,) = call(scan_kernel, [slices], 2, 1 << 20)(states, swap_cores(states))
    prior = lax.all_to_all(priors, PLANE, 0, 0, tiled=True).reshape(STATE)
    (intra,) = call(intra_kernel, [(SQUARE, F32)], 3, 1 << 30)(queries, keys, values)
    gain_row = gain.reshape(1, WIDTH)
    att, gated = call(norm_kernel, [(SQUARE, F32), (SQUARE, BF)], 4, 1 << 28)(
        queries, gain_row, intra, prior
    )
    gated_mate = swap_cores(gated)

    quarter, eighth = ((4, WIDTH, 128), BF), ((4, WIDTH // 2, 128), BF)
    near, far, part, up, down, low, high = call(
        main_kernel,
        [(SQUARE, F32), (SQUARE, BF), quarter, quarter, quarter, eighth, eighth],
        13,
        1 << 33,
        0,
        [pltpu.VMEM(SQUARE, BF), pltpu.VMEM(SQUARE, F32)],
    )(*chunks, gated, gated_mate, weight)
    product_mate = swap_cores(far)
    up, down = call(relay_kernel, [quarter, quarter], 4, 1 << 20)(
        up, down, shift(low, "dp", 4, 1), shift(high, "dp", 4, -1)
    )
    block = (WIDTH, 128)
    part, up, away, down = call(
        column_kernel, [(block, F32), (block, BF), (block, BF), (block, BF)], 3, 1 << 20
    )(part, shift(up, "dp", 4, 1), shift(down, "dp", 4, -1))
    (weight_grad,) = call(sum_kernel, [((128, WIDTH), F32)], 4, 1 << 20)(
        part, shift(up, "y", 4, 1), shift(away, "y", 4, 2), shift(down, "y", 4, -1)
    )
    ga, send = call(grad_kernel, [(SQUARE, BF), (STATE_GAIN, BF)], 5, 1 << 29)(
        near, product_mate, queries, att, gain_row
    )
    total, after = call(row_back_kernel, [(STATE_GAIN, BF), (STATE, F32)], 4, 1 << 22)(
        send, *[shift(send, "dp", 4, -k) for k in (1, 2, 3)]
    )
    other = swap_cores(total)
    (both,) = call(pair_back_kernel, [(STATE_GAIN, BF)], 2, 1 << 22)(total, other)
    upper = [shift(both, "y", 4, -k) for k in (1, 2, 3)]
    query_grad, key_part, value_part = call(
        post_kernel, [(SQUARE, BF), (SQUARE, F32), (SQUARE, F32)], 5, 1 << 31
    )(queries, keys, values, ga, prior)
    key_grad, value_grad, gain_sum = call(
        final_kernel, [(SQUARE, BF), (SQUARE, BF), ((16, HEAD_DIM), F32)], 10, 1 << 28
    )(keys, values, key_part, value_part, after, other, both, *upper)
    gain_grad = (gain_sum[0:4] + gain_sum[4:8]).reshape(WIDTH)
    return query_grad, key_grad, value_grad, gain_grad, weight_grad


def solution(mesh):
    grid = Mesh(mesh.devices.reshape(4, 2, RING, 4), ("y", "core", "tp", "dp"))
    rows = P(("y", "core", "dp"), "tp")
    return jax.shard_map(
        body,
        mesh=grid,
        in_specs=(rows, rows, rows, P("tp"), rows, rows),
        out_specs=(rows, rows, rows, P("tp"), rows),
        check_vma=False,
    )
```

time: 364 us -> 155 us (0.43)
  the two profiles are of different devices: /device:TPU:6 before, /device:TPU:32 now
where the time goes in v2:
time: 155 us
  waiting for transfers between devices  62.9 us (41%)
  starting transfers between devices  58.1 us (37%)
  Pallas kernels  18.8 us (12%)
  local copies, waits for them, and re-layouts  13.3 us (9%)
    ppermute x13, waiting for transfers between devices, shift(): return lax.ppermute(x, axis, pairs)  25.3 us
    ppermute x8, waiting for transfers between devices, ring_step(): return lax.ppermute(x, ('core', 'tp'), pairs)  24 us
    ppermute x8, starting transfers between devices, ring_step(): return lax.ppermute(x, ('core', 'tp'), pairs)  20.9 us
    ppermute x13, starting transfers between devices, shift(): return lax.ppermute(x, axis, pairs)  17.7 us
    unnamed x37, local copies, waits for them, and re-layouts  11.1 us
    pallas_call x1, Pallas kernels, body(): call(main_kernel, [(SQUARE, F32), (SQUARE, BF), quarter, quarter, quarter...  7.87 us
    all_to_all x1, waiting for transfers between devices, body(): weight = lax.all_to_all(spread, PLANE, 0, 0, tiled=True)  7.81 us
    all_to_all x1, starting transfers between devices, body(): weight = lax.all_to_all(spread, PLANE, 0, 0, tiled=True)  7.16 us
  transfers between devices with their start and end apart: 28, of which 14 were waited for; matrix products, arithmetic and copies ran while one was open for 1% of the time, Pallas kernels for 6%

profile of v2, /device:TPU:32, one launch (start us, length us, event | category | flops | bytes accessed | tf_op | source)
XLA Modules:
  0.0 154.5 jit_solution(11682830747917947883)
XLA Ops:
  7.3 7.2 %all-to-all-start = ((bf16[16,144,512]{2,1,0:T(8,128)(2,1)}), bf16[16,144,512]{2,1,0:T(8,128)(2,1)S(1)}, u32[]{:S(2)}, u32[]{:S(2)}) async-start(bf16[16,144,512]{2,1,0:T(8,128)(2,1)} %copy-done), calls=%async_computation | async-start | bytes 4718592 | tf_op jit(solution)/shard_map/all_to_all | solution.py:304
  18.1 14.2 %collective-permute-done.2.refs_3_ = bf16[1024,512]{1,0:T(8,128)(2,1)} collective-permute-done((bf16[1024,512]{1,0:T(8,128)(2,1)S(1)}, bf16[1024,512]{1,0:T(8,128)(2,1)}, u32[]{:S(2)}, u32[]{:S(2)}) %collective-permute-start.2) | collective-permute-done | bytes 1048608 | tf_op jit(solution)/shard_map/ppermute | solution.py:290
  32.3 6.3 %collective-permute-start.4 = (bf16[1024,512]{1,0:T(8,128)(2,1)}, bf16[1024,512]{1,0:T(8,128)(2,1)}, u32[]{:S(2)}, u32[]{:S(2)}) collective-permute-start(bf16[1024,512]{1,0:T(8,128)(2,1)} %collective-permute-done.2.refs_3_), channel_id=1, source_target_pairs={{32,60},{4,0},{40,36},{12,8},{48,44},{20,16},{56,52},{28,24},{33,6... | collective-permute-start | bytes 3145736 | tf_op jit(solution)/shard_map/ppermute | solution.py:290
  38.6 2.3 %collective-permute-start.3 = (bf16[1024,512]{1,0:T(8,128)(2,1)}, bf16[1024,512]{1,0:T(8,128)(2,1)}, u32[]{:S(2)}, u32[]{:S(2)}) collective-permute-start(bf16[1024,512]{1,0:T(8,128)(2,1)} %collective-permute-done.1.refs_2_), channel_id=1, source_target_pairs={{32,36},{4,8},{40,44},{12,16},{48,52},{20,24},{56,60},{28,0},{33,3... | collective-permute-start | bytes 3145736 | tf_op jit(solution)/shard_map/ppermute | solution.py:290
  40.9 7.8 %all-to-all-done.in_ref.refs_12_ = bf16[16,144,512]{2,1,0:T(8,128)(2,1)S(1)} async-done(((bf16[16,144,512]{2,1,0:T(8,128)(2,1)}), bf16[16,144,512]{2,1,0:T(8,128)(2,1)S(1)}, u32[]{:S(2)}, u32[]{:S(2)}) %all-to-all-start) | async-done | bytes 2359328 | tf_op jit(solution)/shard_map/all_to_all | solution.py:304
  50.2 2.3 %collective-permute-done.3.refs_0_ = bf16[1024,512]{1,0:T(8,128)(2,1)} collective-permute-done((bf16[1024,512]{1,0:T(8,128)(2,1)}, bf16[1024,512]{1,0:T(8,128)(2,1)}, u32[]{:S(2)}, u32[]{:S(2)}) %collective-permute-start.3) | collective-permute-done | bytes 1048608 | tf_op jit(solution)/shard_map/ppermute | solution.py:290
  55.2 5.6 %collective-permute-start.9 = (bf16[16,32,128]{2,1,0:T(8,128)(2,1)}, bf16[16,32,128]{2,1,0:T(8,128)(2,1)S(1)}, u32[]{:S(2)}, u32[]{:S(2)}) collective-permute-start(bf16[16,32,128]{2,1,0:T(8,128)(2,1)} %copy-done.8), channel_id=1, source_target_pairs={{0,32},{32,0},{1,33},{33,1},{2,34},{34,2},{3,35},{35,3},{4,36},{36... | collective-permute-start | bytes 393224 | tf_op jit(solution)/shard_map/ppermute | solution.py:282
  63.6 4.0 %all-to-all-start.1 = ((bf16[16,32,128]{2,1,0:T(8,128)(2,1)}), bf16[16,32,128]{2,1,0:T(8,128)(2,1)S(1)}, u32[]{:S(2)}, u32[]{:S(2)}) async-start(bf16[16,32,128]{2,1,0:T(8,128)(2,1)} %shard_map.105), calls=%async_computation.1 | async-start | bytes 262144 | tf_op jit(solution)/shard_map/all_to_all | solution.py:319
  71.1 4.6 %all-to-all-done.1 = bf16[16,32,128]{2,1,0:T(8,128)(2,1)S(1)} async-done(((bf16[16,32,128]{2,1,0:T(8,128)(2,1)}), bf16[16,32,128]{2,1,0:T(8,128)(2,1)S(1)}, u32[]{:S(2)}, u32[]{:S(2)}) %all-to-all-start.1) | async-done | bytes 131104 | tf_op jit(solution)/shard_map/all_to_all | solution.py:319
  79.8 4.3 %collective-permute-start.7 = (bf16[512,512]{1,0:T(8,128)(2,1)S(1)}, bf16[512,512]{1,0:T(8,128)(2,1)S(1)}, u32[]{:S(2)}, u32[]{:S(2)}) collective-permute-start(bf16[512,512]{1,0:T(8,128)(2,1)S(1)} %slice.16), channel_id=1, source_target_pairs={{32,36},{4,8},{40,44},{12,16},{48,52},{20,24},{56,60},{28,0},{33,3... | collective-permute-start | bytes 1572872 | tf_op jit(solution)/shard_map/ppermute | solution.py:290
  85.2 2.6 %collective-permute-start.8 = (bf16[512,512]{1,0:T(8,128)(2,1)S(1)}, bf16[512,512]{1,0:T(8,128)(2,1)S(1)}, u32[]{:S(2)}, u32[]{:S(2)}) collective-permute-start(bf16[512,512]{1,0:T(8,128)(2,1)S(1)} %slice.17), channel_id=1, source_target_pairs={{32,60},{4,0},{40,36},{12,8},{48,44},{20,16},{56,52},{28,24},{33,6... | collective-permute-start | bytes 1572872 | tf_op jit(solution)/shard_map/ppermute | solution.py:290
  87.8 2.9 %collective-permute-done.7.refs_8_ = bf16[512,512]{1,0:T(8,128)(2,1)S(1)} collective-permute-done((bf16[512,512]{1,0:T(8,128)(2,1)S(1)}, bf16[512,512]{1,0:T(8,128)(2,1)S(1)}, u32[]{:S(2)}, u32[]{:S(2)}) %collective-permute-start.7) | collective-permute-done | bytes 524320 | tf_op jit(solution)/shard_map/ppermute | solution.py:290
  90.8 3.7 %collective-permute-done.8.refs_9_ = bf16[512,512]{1,0:T(8,128)(2,1)S(1)} collective-permute-done((bf16[512,512]{1,0:T(8,128)(2,1)S(1)}, bf16[512,512]{1,0:T(8,128)(2,1)S(1)}, u32[]{:S(2)}, u32[]{:S(2)}) %collective-permute-start.8) | collective-permute-done | bytes 524320 | tf_op jit(solution)/shard_map/ppermute | solution.py:290
  94.5 7.9 %shard_map.107 = (f32[512,512]{1,0:T(8,128)S(1)}, bf16[512,512]{1,0:T(8,128)(2,1)S(1)}, bf16[4,512,128]{2,1,0:T(8,128)(2,1)S(1)}, bf16[4,512,128]{2,1,0:T(8,128)...) custom-call(bf16[512,512]{1,0:T(8,128)(2,1)S(1)} %copy-done.13, ...), custom_call_target="tpu_custom_call" | custom-call | flops 8589934592 | bytes 4194304 | tf_op jit(solution)/shard_map/pallas_call | solution.py:328
  103.2 2.7 %collective-permute-start.20 = (bf16[4,256,128]{2,1,0:T(8,128)(2,1)S(1)}, bf16[4,256,128]{2,1,0:T(8,128)(2,1)S(1)}, u32[]{:S(2)}, u32[]{:S(2)}) collective-permute-start(bf16[4,256,128]{2,1,0:T(8,128)(2,1)S(1)} %get-tuple-element.52), channel_id=1, source_target_pairs={{0,3},{1,0},{2,1},{3,2},{4,7},{5,4},{6,5},{7,6},{8,11},{9,8},{10,9... | collective-permute-start | bytes 786440 | tf_op jit(solution)/shard_map/ppermute | solution.py:278
  106.6 6.1 %collective-permute-done.19.low_ref = bf16[4,256,128]{2,1,0:T(8,128)(2,1)S(1)} collective-permute-done((bf16[4,256,128]{2,1,0:T(8,128)(2,1)S(1)}, bf16[4,256,128]{2,1,0:T(8,128)(2,1)S(1)}, u32[]{:S(2)}, u32[]{:S(2)}) %collective-permute-start.19) | collective-permute-done | bytes 262176 | tf_op jit(solution)/shard_map/ppermute | solution.py:278
  113.1 3.4 %collective-permute-start.22 = (bf16[4,512,128]{2,1,0:T(8,128)(2,1)S(1)}, bf16[4,512,128]{2,1,0:T(8,128)(2,1)S(1)}, u32[]{:S(2)}, u32[]{:S(2)}) collective-permute-start(bf16[4,512,128]{2,1,0:T(8,128)(2,1)S(1)} %get-tuple-element.54), channel_id=1, source_target_pairs={{0,3},{1,0},{2,1},{3,2},{4,7},{5,4},{6,5},{7,6},{8,11},{9,8},{10,9... | collective-permute-start | bytes 1572872 | tf_op jit(solution)/shard_map/ppermute | solution.py:278
  117.7 3.4 %collective-permute-start.13 = (bf16[528,128]{1,0:T(8,128)(2,1)S(1)}, bf16[528,128]{1,0:T(8,128)(2,1)S(1)}, u32[]{:S(2)}, u32[]{:S(2)}) collective-permute-start(bf16[528,128]{1,0:T(8,128)(2,1)S(1)} %get-tuple-element.42.own_ref), channel_id=1, source_target_pairs={{0,2},{1,3},{2,0},{3,1},{4,6},{5,7},{6,4},{7,5},{8,10},{9,11},{10,... | collective-permute-start | bytes 405512 | tf_op jit(solution)/shard_map/ppermute | solution.py:278
  121.7 9.8 %collective-permute-done.14.r3_ref = bf16[528,128]{1,0:T(8,128)(2,1)S(1)} collective-permute-done((bf16[528,128]{1,0:T(8,128)(2,1)S(1)}, bf16[528,128]{1,0:T(8,128)(2,1)S(1)}, u32[]{:S(2)}, u32[]{:S(2)}) %collective-permute-start.14) | collective-permute-done | bytes 135200 | tf_op jit(solution)/shard_map/ppermute | solution.py:278
  131.5 4.1 %collective-permute-done.13.r2_ref = bf16[528,128]{1,0:T(8,128)(2,1)S(1)} collective-permute-done((bf16[528,128]{1,0:T(8,128)(2,1)S(1)}, bf16[528,128]{1,0:T(8,128)(2,1)S(1)}, u32[]{:S(2)}, u32[]{:S(2)}) %collective-permute-start.13) | collective-permute-done | bytes 135200 | tf_op jit(solution)/shard_map/ppermute | solution.py:278
  136.4 2.1 %collective-permute-start.24 = (bf16[512,128]{1,0:T(8,128)(2,1)S(1)}, bf16[512,128]{1,0:T(8,128)(2,1)S(1)}, u32[]{:S(2)}, u32[]{:S(2)}) collective-permute-start(bf16[512,128]{1,0:T(8,128)(2,1)S(1)} %get-tuple-element.57), channel_id=1, source_target_pairs={{0,128},{64,192},{128,0},{192,64},{1,129},{65,193},{129,1},{193,65... | collective-permute-start | bytes 393224 | tf_op jit(solution)/shard_map/ppermute | solution.py:278
  140.6 1.9 %collective-permute-start.17 = (bf16[528,128]{1,0:T(8,128)(2,1)S(1)}, bf16[528,128]{1,0:T(8,128)(2,1)S(1)}, u32[]{:S(2)}, u32[]{:S(2)}) collective-permute-start(bf16[528,128]{1,0:T(8,128)(2,1)S(1)} %shard_map.111.own), channel_id=1, source_target_pairs={{0,128},{64,192},{128,0},{192,64},{1,129},{65,193},{129,1},{193,65... | collective-permute-start | bytes 405512 | tf_op jit(solution)/shard_map/ppermute | solution.py:278
  142.5 3.9 %collective-permute-done.23.r1_ref = bf16[512,128]{1,0:T(8,128)(2,1)S(1)} collective-permute-done((bf16[512,128]{1,0:T(8,128)(2,1)S(1)}, bf16[512,128]{1,0:T(8,128)(2,1)S(1)}, u32[]{:S(2)}, u32[]{:S(2)}) %collective-permute-start.23) | collective-permute-done | bytes 131104 | tf_op jit(solution)/shard_map/ppermute | solution.py:278
  146.5 3.8 %shard_map.109 = (bf16[512,512]{1,0:T(8,128)(2,1)}, f32[512,512]{1,0:T(8,128)S(1)}, f32[512,512]{1,0:T(8,128)S(1)}) custom-call(bf16[512,512]{1,0:T(8,128)(2,1)S(1)} %copy-done.7, bf16[512,512]{1,0:T(8,128)(2,1)S(1)} %copy-done.2, bf16[512,512]{1,0:T(8,128)(2,1)S(1)} %copy-done.4, bf16[512,512]{1,0:T(8,128)(2,1)S(1)} %get-tuple-element.38.ga_ref, ...), custom_call_target="tpu_custom_call" | custom-call | flops 2147483648 | bytes 4194304 | tf_op jit(solution)/shard_map/pallas_call | solution.py:356
  (88 shorter events, 36.7 us)
Async XLA Ops:
  0.6 13.9 %collective-permute-start = (bf16[512,512]{1,0:T(8,128)(2,1)}, bf16[512,512]{1,0:T(8,128)(2,1)S(1)}, u32[]{:S(2)}, u32[]{:S(2)}) collective-permute-start(bf16[512,512]{1,0:T(8,128)(2,1)} %refs_0_.1), channel_id=1, source_target_pairs={{32,0},{4,36},{40,8},{12,44},{48,16},{20,52},{56,24},{28,60},{33,1... | collective-permute-start | bytes 1572872 | tf_op jit(solution)/shard_map/ppermute | solution.py:296
  7.3 41.4 %all-to-all-start = ((bf16[16,144,512]{2,1,0:T(8,128)(2,1)}), bf16[16,144,512]{2,1,0:T(8,128)(2,1)S(1)}, u32[]{:S(2)}, u32[]{:S(2)}) async-start(bf16[16,144,512]{2,1,0:T(8,128)(2,1)} %copy-done), calls=%async_computation | async-start | bytes 4718592 | tf_op jit(solution)/shard_map/all_to_all | solution.py:304
  15.4 16.9 %collective-permute-start.2 = (bf16[1024,512]{1,0:T(8,128)(2,1)S(1)}, bf16[1024,512]{1,0:T(8,128)(2,1)}, u32[]{:S(2)}, u32[]{:S(2)}) collective-permute-start(bf16[1024,512]{1,0:T(8,128)(2,1)S(1)} %constant_dynamic-update-slice_fusion), channel_id=1, source_target_pairs={{0,28},{36,32},{8,4},{44,40},{16,12},{52,48},{24,20},{60,56},{1,29... | collective-permute-start | bytes 3145736 | tf_op jit(solution)/shard_map/ppermute | solution.py:290
  16.8 21.8 %collective-permute-start.1 = (bf16[1024,512]{1,0:T(8,128)(2,1)S(1)}, bf16[1024,512]{1,0:T(8,128)(2,1)}, u32[]{:S(2)}, u32[]{:S(2)}) collective-permute-start(bf16[1024,512]{1,0:T(8,128)(2,1)S(1)} %constant_dynamic-update-slice_fusion), channel_id=1, source_target_pairs={{0,4},{36,40},{8,12},{44,48},{16,20},{52,56},{24,28},{60,32},{1,5}... | collective-permute-start | bytes 3145736 | tf_op jit(solution)/shard_map/ppermute | solution.py:290
  32.3 17.9 %collective-permute-start.4 = (bf16[1024,512]{1,0:T(8,128)(2,1)}, bf16[1024,512]{1,0:T(8,128)(2,1)}, u32[]{:S(2)}, u32[]{:S(2)}) collective-permute-start(bf16[1024,512]{1,0:T(8,128)(2,1)} %collective-permute-done.2.refs_3_), channel_id=1, source_target_pairs={{32,60},{4,0},{40,36},{12,8},{48,44},{20,16},{56,52},{28,24},{33,6... | collective-permute-start | bytes 3145736 | tf_op jit(solution)/shard_map/ppermute | solution.py:290
  38.6 13.9 %collective-permute-start.3 = (bf16[1024,512]{1,0:T(8,128)(2,1)}, bf16[1024,512]{1,0:T(8,128)(2,1)}, u32[]{:S(2)}, u32[]{:S(2)}) collective-permute-start(bf16[1024,512]{1,0:T(8,128)(2,1)} %collective-permute-done.1.refs_2_), channel_id=1, source_target_pairs={{32,36},{4,8},{40,44},{12,16},{48,52},{20,24},{56,60},{28,0},{33,3... | collective-permute-start | bytes 3145736 | tf_op jit(solution)/shard_map/ppermute | solution.py:290
  52.5 26.2 %collective-permute-start.5 = (bf16[1024,512]{1,0:T(8,128)(2,1)}, bf16[1024,512]{1,0:T(8,128)(2,1)}, u32[]{:S(2)}, u32[]{:S(2)}) collective-permute-start(bf16[1024,512]{1,0:T(8,128)(2,1)} %get-tuple-element.32.refs_4_), channel_id=1, source_target_pairs={{0,4},{36,40},{8,12},{44,48},{16,20},{52,56},{24,28},{60,32},{1,5}... | collective-permute-start | bytes 3145736 | tf_op jit(solution)/shard_map/ppermute | solution.py:290
  53.9 30.2 %collective-permute-start.6 = (bf16[1024,512]{1,0:T(8,128)(2,1)}, bf16[1024,512]{1,0:T(8,128)(2,1)}, u32[]{:S(2)}, u32[]{:S(2)}) collective-permute-start(bf16[1024,512]{1,0:T(8,128)(2,1)} %get-tuple-element.33.refs_5_), channel_id=1, source_target_pairs={{0,28},{36,32},{8,4},{44,40},{16,12},{52,48},{24,20},{60,56},{1,29... | collective-permute-start | bytes 3145736 | tf_op jit(solution)/shard_map/ppermute | solution.py:290
  63.6 12.0 %all-to-all-start.1 = ((bf16[16,32,128]{2,1,0:T(8,128)(2,1)}), bf16[16,32,128]{2,1,0:T(8,128)(2,1)S(1)}, u32[]{:S(2)}, u32[]{:S(2)}) async-start(bf16[16,32,128]{2,1,0:T(8,128)(2,1)} %shard_map.105), calls=%async_computation.1 | async-start | bytes 262144 | tf_op jit(solution)/shard_map/all_to_all | solution.py:319
  79.8 11.0 %collective-permute-start.7 = (bf16[512,512]{1,0:T(8,128)(2,1)S(1)}, bf16[512,512]{1,0:T(8,128)(2,1)S(1)}, u32[]{:S(2)}, u32[]{:S(2)}) collective-permute-start(bf16[512,512]{1,0:T(8,128)(2,1)S(1)} %slice.16), channel_id=1, source_target_pairs={{32,36},{4,8},{40,44},{12,16},{48,52},{20,24},{56,60},{28,0},{33,3... | collective-permute-start | bytes 1572872 | tf_op jit(solution)/shard_map/ppermute | solution.py:290
  85.2 9.3 %collective-permute-start.8 = (bf16[512,512]{1,0:T(8,128)(2,1)S(1)}, bf16[512,512]{1,0:T(8,128)(2,1)S(1)}, u32[]{:S(2)}, u32[]{:S(2)}) collective-permute-start(bf16[512,512]{1,0:T(8,128)(2,1)S(1)} %slice.17), channel_id=1, source_target_pairs={{32,60},{4,0},{40,36},{12,8},{48,44},{20,16},{56,52},{28,24},{33,6... | collective-permute-start | bytes 1572872 | tf_op jit(solution)/shard_map/ppermute | solution.py:290
  102.4 10.3 %collective-permute-start.19 = (bf16[4,256,128]{2,1,0:T(8,128)(2,1)S(1)}, bf16[4,256,128]{2,1,0:T(8,128)(2,1)S(1)}, u32[]{:S(2)}, u32[]{:S(2)}) collective-permute-start(bf16[4,256,128]{2,1,0:T(8,128)(2,1)S(1)} %get-tuple-element.51), channel_id=1, source_target_pairs={{0,1},{1,2},{2,3},{3,0},{4,5},{5,6},{6,7},{7,4},{8,9},{9,10},{10,1... | collective-permute-start | bytes 786440 | tf_op jit(solution)/shard_map/ppermute | solution.py:278
  103.2 9.5 %collective-permute-start.20 = (bf16[4,256,128]{2,1,0:T(8,128)(2,1)S(1)}, bf16[4,256,128]{2,1,0:T(8,128)(2,1)S(1)}, u32[]{:S(2)}, u32[]{:S(2)}) collective-permute-start(bf16[4,256,128]{2,1,0:T(8,128)(2,1)S(1)} %get-tuple-element.52), channel_id=1, source_target_pairs={{0,3},{1,0},{2,1},{3,2},{4,7},{5,4},{6,5},{7,6},{8,11},{9,8},{10,9... | collective-permute-start | bytes 786440 | tf_op jit(solution)/shard_map/ppermute | solution.py:278
  105.9 10.7 %collective-permute-start.11 = (bf16[512,512]{1,0:T(8,128)(2,1)S(1)}, bf16[512,512]{1,0:T(8,128)(2,1)S(1)}, u32[]{:S(2)}, u32[]{:S(2)}) collective-permute-start(bf16[512,512]{1,0:T(8,128)(2,1)S(1)} %get-tuple-element.36), channel_id=1, source_target_pairs={{0,32},{32,0},{1,33},{33,1},{2,34},{34,2},{3,35},{35,3},{4,36},{36... | collective-permute-start | bytes 1572872 | tf_op jit(solution)/shard_map/ppermute | solution.py:282
  112.8 23.0 %collective-permute-start.21 = (bf16[4,512,128]{2,1,0:T(8,128)(2,1)S(1)}, bf16[4,512,128]{2,1,0:T(8,128)(2,1)S(1)}, u32[]{:S(2)}, u32[]{:S(2)}) collective-permute-start(bf16[4,512,128]{2,1,0:T(8,128)(2,1)S(1)} %get-tuple-element.53), channel_id=1, source_target_pairs={{0,1},{1,2},{2,3},{3,0},{4,5},{5,6},{6,7},{7,4},{8,9},{9,10},{10,1... | collective-permute-start | bytes 1572872 | tf_op jit(solution)/shard_map/ppermute | solution.py:278
  113.1 22.7 %collective-permute-start.22 = (bf16[4,512,128]{2,1,0:T(8,128)(2,1)S(1)}, bf16[4,512,128]{2,1,0:T(8,128)(2,1)S(1)}, u32[]{:S(2)}, u32[]{:S(2)}) collective-permute-start(bf16[4,512,128]{2,1,0:T(8,128)(2,1)S(1)} %get-tuple-element.54), channel_id=1, source_target_pairs={{0,3},{1,0},{2,1},{3,2},{4,7},{5,4},{6,5},{7,6},{8,11},{9,8},{10,9... | collective-permute-start | bytes 1572872 | tf_op jit(solution)/shard_map/ppermute | solution.py:278
  117.6 13.9 %collective-permute-start.14 = (bf16[528,128]{1,0:T(8,128)(2,1)S(1)}, bf16[528,128]{1,0:T(8,128)(2,1)S(1)}, u32[]{:S(2)}, u32[]{:S(2)}) collective-permute-start(bf16[528,128]{1,0:T(8,128)(2,1)S(1)} %get-tuple-element.42.own_ref), channel_id=1, source_target_pairs={{0,1},{1,2},{2,3},{3,0},{4,5},{5,6},{6,7},{7,4},{8,9},{9,10},{10,1... | collective-permute-start | bytes 405512 | tf_op jit(solution)/shard_map/ppermute | solution.py:278
  117.7 17.9 %collective-permute-start.13 = (bf16[528,128]{1,0:T(8,128)(2,1)S(1)}, bf16[528,128]{1,0:T(8,128)(2,1)S(1)}, u32[]{:S(2)}, u32[]{:S(2)}) collective-permute-start(bf16[528,128]{1,0:T(8,128)(2,1)S(1)} %get-tuple-element.42.own_ref), channel_id=1, source_target_pairs={{0,2},{1,3},{2,0},{3,1},{4,6},{5,7},{6,4},{7,5},{8,10},{9,11},{10,... | collective-permute-start | bytes 405512 | tf_op jit(solution)/shard_map/ppermute | solution.py:278
  121.1 14.5 %collective-permute-start.12 = (bf16[528,128]{1,0:T(8,128)(2,1)S(1)}, bf16[528,128]{1,0:T(8,128)(2,1)S(1)}, u32[]{:S(2)}, u32[]{:S(2)}) collective-permute-start(bf16[528,128]{1,0:T(8,128)(2,1)S(1)} %get-tuple-element.42.own_ref), channel_id=1, source_target_pairs={{0,3},{1,0},{2,1},{3,2},{4,7},{5,4},{6,5},{7,6},{8,11},{9,8},{10,9... | collective-permute-start | bytes 405512 | tf_op jit(solution)/shard_map/ppermute | solution.py:278
  136.1 10.4 %collective-permute-start.23 = (bf16[512,128]{1,0:T(8,128)(2,1)S(1)}, bf16[512,128]{1,0:T(8,128)(2,1)S(1)}, u32[]{:S(2)}, u32[]{:S(2)}) collective-permute-start(bf16[512,128]{1,0:T(8,128)(2,1)S(1)} %get-tuple-element.56), channel_id=1, source_target_pairs={{0,64},{64,128},{128,192},{192,0},{1,65},{65,129},{129,193},{193,1... | collective-permute-start | bytes 393224 | tf_op jit(solution)/shard_map/ppermute | solution.py:278
  136.4 13.9 %collective-permute-start.24 = (bf16[512,128]{1,0:T(8,128)(2,1)S(1)}, bf16[512,128]{1,0:T(8,128)(2,1)S(1)}, u32[]{:S(2)}, u32[]{:S(2)}) collective-permute-start(bf16[512,128]{1,0:T(8,128)(2,1)S(1)} %get-tuple-element.57), channel_id=1, source_target_pairs={{0,128},{64,192},{128,0},{192,64},{1,129},{65,193},{129,1},{193,65... | collective-permute-start | bytes 393224 | tf_op jit(solution)/shard_map/ppermute | solution.py:278
  138.5 11.8 %collective-permute-start.25 = (bf16[512,128]{1,0:T(8,128)(2,1)S(1)}, bf16[512,128]{1,0:T(8,128)(2,1)S(1)}, u32[]{:S(2)}, u32[]{:S(2)}) collective-permute-start(bf16[512,128]{1,0:T(8,128)(2,1)S(1)} %get-tuple-element.58), channel_id=1, source_target_pairs={{0,192},{64,0},{128,64},{192,128},{1,193},{65,1},{129,65},{193,129... | collective-permute-start | bytes 393224 | tf_op jit(solution)/shard_map/ppermute | solution.py:278
  139.7 12.2 %collective-permute-start.18 = (bf16[528,128]{1,0:T(8,128)(2,1)S(1)}, bf16[528,128]{1,0:T(8,128)(2,1)S(1)}, u32[]{:S(2)}, u32[]{:S(2)}) collective-permute-start(bf16[528,128]{1,0:T(8,128)(2,1)S(1)} %shard_map.111.own), channel_id=1, source_target_pairs={{0,64},{64,128},{128,192},{192,0},{1,65},{65,129},{129,193},{193,1... | collective-permute-start | bytes 405512 | tf_op jit(solution)/shard_map/ppermute | solution.py:278
  140.6 11.2 %collective-permute-start.17 = (bf16[528,128]{1,0:T(8,128)(2,1)S(1)}, bf16[528,128]{1,0:T(8,128)(2,1)S(1)}, u32[]{:S(2)}, u32[]{:S(2)}) collective-permute-start(bf16[528,128]{1,0:T(8,128)(2,1)S(1)} %shard_map.111.own), channel_id=1, source_target_pairs={{0,128},{64,192},{128,0},{192,64},{1,129},{65,193},{129,1},{193,65... | collective-permute-start | bytes 405512 | tf_op jit(solution)/shard_map/ppermute | solution.py:278
  (22 other events, 236.3 us)
